TPU v7x, 128 devices: a whole 4x4x4 slice. The times are simulated.
128 devices in a mesh: row: 16 (over y, x), col: 8 (over z, core).
Axes of the slice: x: 4, y: 4, z: 4, core: 2. Of those that a mesh axis runs over, the one named last changes fastest.
Arguments:
- alignment_features: bfloat16 [1024, 1024, 256], P(('row', 'col')), may hold values from -6 to 6
- standardize_gain: float32 [256], replicated, may hold values from 0.25 to 1.75
- standardize_offset: float32 [256], replicated, may hold values from -3 to 3
- first_factor_matrix: bfloat16 [256, 32], replicated, may hold values from -0.375 to 0.375
- first_factor_offset: float32 [32], replicated, may hold values from -3 to 3
- second_factor_matrix: bfloat16 [256, 32], replicated, may hold values from -0.375 to 0.375
- second_factor_offset: float32 [32], replicated, may hold values from -3 to 3
- final_matrix: bfloat16 [1024, 128], replicated, may hold values from -1 to 1
- final_offset: float32 [128], replicated, may hold values from -3 to 3
- pairwise_features: bfloat16 [1024, 1024, 128], P('row', 'col'), may hold values from -6 to 6
Outputs:
- pair_out: bfloat16 [1024, 1024, 128], P('row', 'col')
All inputs are finite; a program needn't handle non-finite values.
Results may differ from a plain program's by a relative error of at most 0.005.
Values may be sent and summed in bfloat16 or wider, within the bound.
No kernel may reach another device: no remote copies, remote signals or barrier semaphores. Data moves between devices by JAX's collectives and lax.ppermute only.
A program may use at most 192 MiB of HBM per device.

v0:
```python
import jax
import jax.numpy as jnp
from jax import lax
from jax.sharding import PartitionSpec as P


def per_device(
    alignment_features,
    standardize_gain,
    standardize_offset,
    first_factor_matrix,
    first_factor_offset,
    second_factor_matrix,
    second_factor_offset,
    final_matrix,
    final_offset,
    pairwise_features,
):
    given_entries = alignment_features.astype(jnp.float32)
    mean = jnp.mean(given_entries, axis=-1, keepdims=True)
    centred = given_entries - mean
    variance = jnp.mean(centred * centred, axis=-1, keepdims=True)
    normed = (centred / jnp.sqrt(variance + 1e-05) * standardize_gain + standardize_offset).astype(
        jnp.bfloat16
    )
    left = (
        jnp.einsum("src,cp->srp", normed, first_factor_matrix, preferred_element_type=jnp.float32)
        + first_factor_offset
    ).astype(jnp.bfloat16)
    right = (
        jnp.einsum("src,cp->srp", normed, second_factor_matrix, preferred_element_type=jnp.float32)
        + second_factor_offset
    ).astype(jnp.bfloat16)
    nrows = lax.axis_size("row")
    ncols = lax.axis_size("col")
    shard_alignment_rows = alignment_features.shape[0]
    chain_span = alignment_features.shape[1]
    width = left.shape[2]
    piece = chain_span // (nrows * ncols)
    right_order = right.reshape(shard_alignment_rows, ncols, nrows, piece, width)
    right_order = jnp.transpose(right_order, (0, 2, 1, 3, 4)).reshape(
        shard_alignment_rows, chain_span, width
    )
    left_moved, right_moved = (
        lax.all_to_all(left, ("row", "col"), split_axis=1, concat_axis=0, tiled=True),
        lax.all_to_all(right_order, ("row", "col"), split_axis=1, concat_axis=0, tiled=True),
    )
    left_tile = lax.all_gather(left_moved, "col", axis=1, tiled=True)
    right_tile = lax.all_gather(right_moved, "row", axis=1, tiled=True)
    alignment_span = left_tile.shape[0]
    rows_i = left_tile.shape[1]
    cols_j = right_tile.shape[1]
    channels = pairwise_features.shape[2]
    block = min(16, rows_i)
    count = rows_i // block
    left_blocks = jnp.transpose(
        left_tile.reshape(alignment_span, count, block, width), (1, 0, 2, 3)
    )
    pair_blocks = pairwise_features.reshape(count, block, cols_j, channels)

    def one_block(items):
        left_piece, pair_piece = items
        outer = jnp.einsum(
            "sic,sje->ijce", left_piece, right_tile, preferred_element_type=jnp.float32
        )
        outer = (outer / jnp.float32(alignment_span)).astype(jnp.bfloat16)
        flat = outer.reshape(block * cols_j, width * width)
        update = jnp.dot(flat, final_matrix, preferred_element_type=jnp.float32) + final_offset
        update = update.reshape(block, cols_j, channels)
        return (pair_piece.astype(jnp.float32) + update).astype(jnp.bfloat16)

    result = lax.map(one_block, (left_blocks, pair_blocks))
    return result.reshape(rows_i, cols_j, channels)


def solution(mesh):
    placed = (
        P(("row", "col"), None, None),
        P(),
        P(),
        P(),
        P(),
        P(),
        P(),
        P(),
        P(),
        P("row", "col", None),
    )
    return jax.shard_map(
        per_device, mesh=mesh, in_specs=placed, out_specs=P("row", "col", None), check_vma=False
    )
```

profile of v0, /device:TPU:0, one launch (start us, length us, event | category | flops | bytes accessed | tf_op | source)
XLA Modules:
  0.0 452.4 jit_solution(8044434284686605328)
XLA Ops:
  6.6 3.5 convert_reduce_fusion
  10.1 2.4 fusion.17
  12.6 5.1 %fusion.20 = bf16[8,1024,256]{2,1,0:T(8,128)(2,1)S(1)} fusion(bf16[8,1024,256]{2,1,0:T(8,128)(2,1)S(1)} %copy-done.2, f32[256]{0:T(256)S(1)} %copy-done.5, f32[256]{0:T(256)S(1)} %copy-done.6, f32[8,1024]{1,0:T(8,128)S(1)} %add_sqrt_fusion, f32[8,1024]{1,0:T(8,128)S(1)} %broadcast_multiply_fusion), kind=kLoop, calls=%fused_computation.20 | loop fusion | flops 12582912 | bytes 8456192 | tf_op jit(solution)/shard_map/convert_element_type | solution.py:23
  24.7 24.7 %all_to_all.36 = bf16[128,2,1024]{2,1,0:T(2,128)(2,1)S(1)} all-to-all(bf16[128,2,1024]{2,1,0:T(2,128)(2,1)S(1)} %reshape.48), channel_id=1, replica_groups=mesh['row'=16,'col'=8] {'row','col'}, dimensions={0} | all-to-all | bytes 1048576 | tf_op jit(solution)/shard_map/all_to_all | solution.py:45
  52.5 3.5 fusion.22
  59.0 2.1 reshape.50
  61.1 17.9 %all_to_all.37 = bf16[128,2,1024]{2,1,0:T(2,128)(2,1)S(1)} all-to-all(bf16[128,2,1024]{2,1,0:T(2,128)(2,1)S(1)} %reshape.50), channel_id=1, replica_groups=mesh['row'=16,'col'=8] {'row','col'}, dimensions={0} | all-to-all | bytes 1048576 | tf_op jit(solution)/shard_map/all_to_all | solution.py:46
  82.0 62.3 %all-gather.3.cloned.1.call-done = bf16[1024,64,32]{2,1,0:T(8,128)(2,1)} async-done(((bf16[1024,8,32]{2,1,0:T(8,128)(2,1)}), bf16[1024,64,32]{2,1,0:T(8,128)(2,1)}) %all-gather.3.cloned.1.call-update) | async-done | bytes 4194320 | tf_op jit(solution)/shard_map/all_gather | solution.py:48
  144.3 17.8 %copy.29 = bf16[1024,4,16,32]{0,3,2,1:T(8,128)(2,1)} copy(bf16[1024,4,16,32]{3,2,1,0:T(8,128)(2,1)} %bitcast.70) | data formatting | bytes 8388608 | tf_op jit(solution)/shard_map/reshape | solution.py:57
  162.1 191.6 %all-gather.5.cloned.1.call-done = bf16[1024,128,32]{2,1,0:T(8,128)(2,1)} async-done(((bf16[1024,8,32]{2,1,0:T(8,128)(2,1)}), bf16[1024,128,32]{2,1,0:T(8,128)(2,1)}) %all-gather.5.cloned.1.call-update) | async-done | bytes 8388624 | tf_op jit(solution)/shard_map/all_gather | solution.py:49
  353.7 30.8 %copy.35 = bf16[1024,128,32]{1,0,2:T(8,128)(2,1)} copy(bf16[1024,128,32]{2,1,0:T(8,128)(2,1)} %all-gather.5.cloned.1.call-done) | data formatting | bytes 16777216 | tf_op jit(solution)/shard_map/while | solution.py:72
  384.6 60.3 %while.10 = (s32[]{:T(128)}, bf16[4,16,128,128]{3,2,1,0:T(8,128)(2,1)}, bf16[4,16,128,128]{3,2,1,0:T(8,128)(2,1)}, bf16[4,1024,16,32]{1,3,2,0:T(8,128)(2,1)}, bf...) while((s32[]{:T(128)}, ...), condition=%wide.region_3.4_spmd, body=%wide.region_2.3_spmd.sunk | while | flops 4837081088 | bytes 29623892 | solution.py:72
  384.6 8.2 %fusion.39 = bf16[16,128,32,32]{1,2,3,0:T(8,128)(2,1)S(1)} fusion(bf16[1024,128,32]{1,0,2:T(8,128)(2,1)} %get-tuple-element.134, bf16[4,1024,16,32]{1,3,2,0:T(8,128)(2,1)} %get-tuple-element.133, s32[]{:T(128)} %get-tuple-element.122), kind=kOutput, calls=%fused_computation.3.clone.1 | convolution fusion | flops 4299161600 | bytes 13632000 | tf_op jit(solution)/shard_map/while/body/eval_jaxpr/sic,sje->ijce/dot_general | solution.py:63
  392.8 2.7 copy.51
  395.5 2.1 fusion.40
  399.6 8.2 %fusion.39 = bf16[16,128,32,32]{1,2,3,0:T(8,128)(2,1)S(1)} fusion(bf16[1024,128,32]{1,0,2:T(8,128)(2,1)} %get-tuple-element.134, bf16[4,1024,16,32]{1,3,2,0:T(8,128)(2,1)} %get-tuple-element.133, s32[]{:T(128)} %get-tuple-element.122), kind=kOutput, calls=%fused_computation.3.clone.1 | convolution fusion | flops 4299161600 | bytes 13632000 | tf_op jit(solution)/shard_map/while/body/eval_jaxpr/sic,sje->ijce/dot_general | solution.py:63
  407.9 2.7 copy.51
  410.6 2.1 fusion.40
  414.7 8.2 %fusion.39 = bf16[16,128,32,32]{1,2,3,0:T(8,128)(2,1)S(1)} fusion(bf16[1024,128,32]{1,0,2:T(8,128)(2,1)} %get-tuple-element.134, bf16[4,1024,16,32]{1,3,2,0:T(8,128)(2,1)} %get-tuple-element.133, s32[]{:T(128)} %get-tuple-element.122), kind=kOutput, calls=%fused_computation.3.clone.1 | convolution fusion | flops 4299161600 | bytes 13632000 | tf_op jit(solution)/shard_map/while/body/eval_jaxpr/sic,sje->ijce/dot_general | solution.py:63
  422.9 2.7 copy.51
  425.6 2.1 fusion.40
  429.8 8.2 %fusion.39 = bf16[16,128,32,32]{1,2,3,0:T(8,128)(2,1)S(1)} fusion(bf16[1024,128,32]{1,0,2:T(8,128)(2,1)} %get-tuple-element.134, bf16[4,1024,16,32]{1,3,2,0:T(8,128)(2,1)} %get-tuple-element.133, s32[]{:T(128)} %get-tuple-element.122), kind=kOutput, calls=%fused_computation.3.clone.1 | convolution fusion | flops 4299161600 | bytes 13632000 | tf_op jit(solution)/shard_map/while/body/eval_jaxpr/sic,sje->ijce/dot_general | solution.py:63
  438.0 2.7 copy.51
  440.7 2.1 fusion.40
  (43 shorter events, 24.7 us)
Async XLA Ops:
  6.5 13.1 %copy-start = (bf16[256,32]{0,1:T(8,128)(2,1)S(1)}, bf16[256,32]{0,1:T(8,128)(2,1)}, u32[]{:S(2)}) copy-start(bf16[256,32]{0,1:T(8,128)(2,1)} %param.15) | copy-start | bytes 49156
  6.5 6.0 %copy-start.6 = (f32[256]{0:T(256)S(1)}, f32[256]{0:T(256)}, u32[]{:S(2)}) copy-start(f32[256]{0:T(256)} %param.13) | copy-start | bytes 3076
  6.5 6.0 %copy-start.5 = (f32[256]{0:T(256)S(1)}, f32[256]{0:T(256)}, u32[]{:S(2)}) copy-start(f32[256]{0:T(256)} %param.14) | copy-start | bytes 3076
  6.5 137.8 %all-gather.3.cloned.1.call-start = ((), (), s32[]{:S(2)}) async-start(), calls=%async_computation.2 | async-start | bytes 18874368 | tf_op jit(solution)/shard_map/all_gather | solution.py:48
  6.5 3.5 copy-start.2
  12.6 7.1 %copy-start.7 = (f32[32]{0:T(128)S(1)}, f32[32]{0:T(128)}, u32[]{:S(2)}) copy-start(f32[32]{0:T(128)} %param.16) | copy-start | bytes 388
  17.7 2.0 copy-start.3
  49.4 3.1 copy-start.4
  49.4 3.1 copy-start.8
  52.4 301.3 %all-gather.5.cloned.1.call-start = ((), (), s32[]{:S(2)}) async-start(), calls=%async_computation.3 | async-start | bytes 35651584 | tf_op jit(solution)/shard_map/all_gather | solution.py:49
  162.1 222.4 %copy-start.9 = (bf16[1024,128]{1,0:T(8,128)(2,1)S(1)}, bf16[1024,128]{1,0:T(8,128)(2,1)}, u32[]{:S(2)}) copy-start(bf16[1024,128]{1,0:T(8,128)(2,1)} %param.19) | copy-start | bytes 786436
  162.1 222.4 %copy-start.10 = (f32[128]{0:T(128)S(1)}, f32[128]{0:T(128)}, u32[]{:S(2)}) copy-start(f32[128]{0:T(128)} %param.20) | copy-start | bytes 1540
  444.8 0.7 copy-start.1
Sparse Core Ops, SparseCore 0:
  52.5 91.7 all-gather.2
  146.4 207.2 all-gather.4
where the time goes:
time: 454 us; the launch traced here: 452 us
  waiting for transfers between devices  254 us (56%)
  local copies, waits for them, and re-layouts  76.8 us (17%)
  matrix products  46.2 us (10%)
  blocking collectives  42.6 us (9%)
  other arithmetic  19.1 us (4%)
  between operations  13.6 us (3%)
    all_gather x1, waiting for transfers between devices, per_device(): right_tile = lax.all_gather(right_moved, 'row', axis=1, tiled=True)  192 us
    all_gather x1, waiting for transfers between devices, per_device(): left_tile = lax.all_gather(left_moved, 'col', axis=1, tiled=True)  62.3 us
    dot_general x4, matrix products, one_block(): jnp.einsum('sic,sje->ijce', left_piece, right_tile, preferred_element_typ...  32.9 us
    while x1, local copies, waits for them, and re-layouts, per_device(): result = lax.map(one_block, (left_blocks, pair_blocks))  30.8 us
    all_to_all x1, blocking collectives, per_device(): lax.all_to_all(left, ('row', 'col'), split_axis=1, concat_axis=0, tiled=T...  24.7 us
    all_to_all x1, blocking collectives, per_device(): lax.all_to_all(right_order, ('row', 'col'), split_axis=1, concat_axis=0,...  17.9 us
    reshape x1, local copies, waits for them, and re-layouts, per_device(): left_tile.reshape(alignment_span, count, block, width)  17.8 us
    convert_element_type x4, local copies, waits for them, and re-layouts, one_block(): outer = (outer / jnp.float32(alignment_span)).astype(jnp.bfloat16)  10.8 us
  transfers between devices with their start and end apart: 2, of which 2 were waited for; matrix products, arithmetic and copies ran while one was open for 6% of the time, Pallas kernels for 0%

commit v1 on v0

v1 whole, which is shorter than its diff:
```python
import functools

import jax
import jax.numpy as jnp
from jax import lax
from jax.experimental import pallas as pl
from jax.experimental.pallas import tpu as pltpu
from jax.sharding import PartitionSpec as P

STREAMS = (16, 16)
STEP_ROWS = 16


def project_kernel(x_ref, gain_ref, offset_ref, weights_ref, bias_ref, right_weights_ref, right_bias_ref, out_ref, left, right, flat):
    s = pl.program_id(0)
    x = x_ref[0].astype(jnp.float32)
    mean = jnp.mean(x, axis=-1, keepdims=True)
    centred = x - mean
    variance = jnp.mean(centred * centred, axis=-1, keepdims=True)
    normed = (centred * lax.rsqrt(variance + 1e-05) * gain_ref[...] + offset_ref[...]).astype(jnp.bfloat16)
    flat[...] = jnp.dot(normed, weights_ref[...], preferred_element_type=jnp.float32) + bias_ref[...]
    group = lax.broadcasted_iota(jnp.int32, (256, 128), 1) // 32
    dense = flat[pl.ds(0, 256, stride=4), :]
    for a in range(1, 4):
        dense = jnp.where(group == a, flat[pl.ds(a, 256, stride=4), :], dense)
    left[pl.ds(s, 256, stride=8), :] = dense
    turned = lax.dot_general(
        right_weights_ref[...], normed, (((1,), (1,)), ((), ())), preferred_element_type=jnp.float32
    )
    turned = turned + right_bias_ref[...]
    for cb in range(8):
        right[cb, pl.ds(s, 32, stride=8), :] = turned[:, cb * 128 : (cb + 1) * 128]

    @pl.when(s == pl.num_programs(0) - 1)
    def _():
        for r in range(16):
            for h in range(2):
                rows = left[pl.ds((r * 16 + h * 8) * 8, 64), :].astype(jnp.bfloat16)
                out_ref[h, r * 8 : (r + 1) * 8] = rows.reshape(8, 8, 128)
        for z in range(4):
            for k in range(2):
                rows = right[z * 2 + k].astype(jnp.bfloat16)
                out_ref[k, 128 + z * 32 : 128 + (z + 1) * 32] = rows.reshape(32, 8, 128)


def project(x, gain, offset, first, first_offset, second, second_offset):
    whole = lambda *shape: pl.BlockSpec(shape, lambda s: (0,) * len(shape))
    return pl.pallas_call(
        project_kernel,
        grid=(8,),
        in_specs=[
            pl.BlockSpec((1, 1024, 256), lambda s: (s, 0, 0)),
            whole(1, 256),
            whole(1, 256),
            whole(256, 128),
            whole(1, 128),
            whole(32, 256),
            whole(32, 1),
        ],
        out_specs=whole(2, 256, 8, 128),
        out_shape=jax.ShapeDtypeStruct((2, 256, 8, 128), jnp.bfloat16),
        scratch_shapes=[
            pltpu.VMEM((2048, 128), jnp.float32),
            pltpu.VMEM((8, 256, 128), jnp.float32),
            pltpu.VMEM((1024, 128), jnp.float32),
        ],
        compiler_params=pltpu.CompilerParams(vmem_limit_bytes=32 * 2**20),
        name="project",
    )(
        x,
        gain.reshape(1, 256),
        offset.reshape(1, 256),
        jnp.tile(first, (1, 4)),
        jnp.tile(first_offset, 4).reshape(1, 128),
        second.T,
        second_offset.reshape(32, 1),
    )


def turn_kernel(x_ref, out_ref):
    for place in range(0, 16, 2):
        rows = jnp.concatenate([x_ref[dz, place + d, 0] for d in range(2) for dz in range(4)], axis=0)
        out_ref[:, place * 64 : place * 64 + 128] = jnp.transpose(rows)


def turn(gathered):
    return pl.pallas_call(
        turn_kernel,
        grid=(8,),
        in_specs=[pl.BlockSpec((4, 16, 1, 16, 128), lambda q: (0, 0, q, 0, 0))],
        out_specs=pl.BlockSpec((128, 1024), lambda q: (q, 0)),
        out_shape=jax.ShapeDtypeStruct((1024, 1024), jnp.bfloat16),
        compiler_params=pltpu.CompilerParams(vmem_limit_bytes=16 * 2**20),
        name="turn",
    )(gathered)


def steps_of(part, slot, core):
    bits = [(slot >> b) & 1 for b in range(4)]
    one = lambda lo, hi: (lo * 1) ^ (hi * 3) if core == 0 else (lo * 3) ^ (hi * 1)
    near, far = one(bits[0], bits[1]), one(bits[2], bits[3])
    dx, dy = (near, far) if part == 0 else (far, near)
    return dy * 4 + dx


def product_kernel(depth, first, last, core_ref, own_ref, other_ref, a_lo, a_hi, b_lo, b_hi, weights_ref, *refs):
    refs = list(refs)
    acc_ref = None if first else refs.pop(0)
    pair_ref, offset_ref = (refs.pop(0), refs.pop(0)) if last else (None, None)
    out_ref, left, right, outer, left_sem, right_sem = refs
    half = depth // 2
    b = pl.program_id(0)
    core = core_ref[0]
    rows = STEP_ROWS * 32
    blocks = 1024 // rows

    def left_copy(n):
        source = own_ref if n < blocks else other_ref
        return pltpu.make_async_copy(
            source.at[pl.ds((n % blocks) * rows, rows)], left.at[pl.ds(n * rows, rows)], left_sem.at[n]
        )

    def right_copy(part, slot):
        lo, hi = ((a_lo, a_hi), (b_lo, b_hi))[part]
        source = lo.at[slot] if slot < 8 else hi.at[slot - 8]
        place = jnp.where(core == 0, steps_of(part, slot, 0), steps_of(part, slot, 1))
        to = pl.multiple_of(place * 64, 64)
        return pltpu.make_async_copy(
            source, right.at[pl.ds(part * half, half), pl.ds(to, 64)], right_sem.at[part, slot]
        )

    @pl.when(b == 0)
    def _():
        left_copy(0).start()
        for part in range(2):
            for slot in range(16):
                right_copy(part, slot).start()
        for n in range(1, 2 * blocks):
            left_copy(n).start()

    for n in range(2 * blocks):

        @pl.when(b == n)
        def _():
            left_copy(n).wait()

    block = left[pl.ds(pl.multiple_of(b * rows, rows), rows), :]
    wide = 4 if half % 4 == 0 else 2
    for n in range(depth // wide):
        if (n * wide) % half == 0:

            @pl.when(b == 0)
            def _():
                for slot in range(16):
                    right_copy((n * wide) // half, slot).wait()

        channels = jnp.concatenate([right[n * wide + e] for e in range(wide)], axis=1)
        m = jnp.dot(block, channels, preferred_element_type=jnp.float32).astype(jnp.bfloat16)
        for i in range(STEP_ROWS):
            for e in range(wide):
                outer[i // 2, pl.ds((n * wide + e) * 32, 32), pl.ds((i % 2) * 128, 128)] = m[
                    i * 32 : (i + 1) * 32, e * 128 : (e + 1) * 128
                ]
    for pair in range(STEP_ROWS // 2):
        both = jnp.dot(weights_ref[...], outer[pair], preferred_element_type=jnp.float32)
        for d in range(2):
            i = pair * 2 + d
            update = both[:, d * 128 : (d + 1) * 128]
            if not first:
                update = update + acc_ref[i]
            if last:
                update = jnp.transpose(update) + offset_ref[...] + pair_ref[i].astype(jnp.float32)
            out_ref[i] = update.astype(out_ref.dtype)


def product(depth, core, own, other, pieces, weights, acc, pair, offset):
    blocks = 32 // STEP_ROWS
    tile = pl.BlockSpec(
        (STEP_ROWS, 128, 128), lambda b, core: (((b // blocks) ^ core[0]) * blocks + b % blocks, 0, 0)
    )
    anywhere = pl.BlockSpec(memory_space=pl.ANY)
    operands = [own, other, *pieces, weights]
    specs = [anywhere] * 6 + [pl.BlockSpec((128, depth * 32), lambda b, core: (0, 0))]
    if acc is not None:
        operands.append(acc)
        specs.append(tile)
    last = pair is not None
    if last:
        operands += [pair, offset]
        specs += [tile, pl.BlockSpec((1, 128), lambda b, core: (0, 0))]
    return pl.pallas_call(
        functools.partial(product_kernel, depth, acc is None, last),
        grid_spec=pltpu.PrefetchScalarGridSpec(
            num_scalar_prefetch=1,
            grid=(2 * blocks,),
            in_specs=specs,
            out_specs=tile,
            scratch_shapes=[
                pltpu.VMEM((2048, 1024), jnp.bfloat16),
                pltpu.VMEM((depth, 1024, 128), jnp.bfloat16),
                pltpu.VMEM((STEP_ROWS // 2, depth * 32, 256), jnp.bfloat16),
                pltpu.SemaphoreType.DMA((2 * blocks,)),
                pltpu.SemaphoreType.DMA((2, 16)),
            ],
        ),
        out_shape=jax.ShapeDtypeStruct((64, 128, 128), jnp.bfloat16 if last else jnp.float32),
        compiler_params=pltpu.CompilerParams(vmem_limit_bytes=40 * 2**20),
        name="product",
    )(core, *operands)


def hop(part, step, index):
    row, col = index
    y, x, core = row // 4, row % 4, col % 2
    mask = (1, 3)[(step + core) % 2]
    along_x = (step < 2) == (part == 0)
    return (y * 4 + (x ^ mask), col) if along_x else ((y ^ mask) * 4 + x, col)


def permute(value, to):
    pairs = []
    for row in range(16):
        for col in range(8):
            other = to((row, col))
            pairs.append((row * 8 + col, other[0] * 8 + other[1]))
    return lax.ppermute(value, ("row", "col"), pairs)


def pick(array, index, axis):
    return lax.dynamic_index_in_dim(array, index, axis, keepdims=False)


def per_device(
    alignment_features,
    standardize_gain,
    standardize_offset,
    first_factor_matrix,
    first_factor_offset,
    second_factor_matrix,
    second_factor_offset,
    final_matrix,
    final_offset,
    pairwise_features,
):
    row, col = lax.axis_index("row"), lax.axis_index("col")
    y, x, z, core = row // 4, row % 4, col // 2, col % 2
    projected = project(
        alignment_features,
        standardize_gain,
        standardize_offset,
        first_factor_matrix,
        first_factor_offset,
        second_factor_matrix,
        second_factor_offset,
    )
    mine = pick(projected, core, 0)
    theirs = permute(pick(projected, 1 - core, 0), lambda d: (d[0], d[1] ^ 1))
    merged = jnp.where(
        core == 0, jnp.concatenate([mine, theirs], axis=1), jnp.concatenate([theirs, mine], axis=1)
    )

    right = merged[128:].reshape(4, 32, 16, 128)
    planes = [pick(right, z, 0)] + [
        permute(pick(right, z ^ d, 0), lambda i, d=d: (i[0], ((i[1] // 2) ^ d) * 2 + i[1] % 2)) for d in (1, 2, 3)
    ]
    right = jnp.concatenate(planes, axis=1)

    left = merged[:128].reshape(4, 4, 8, 16, 128)
    left = jnp.stack(
        [pick(left, x, 1)]
        + [permute(pick(left, x ^ d, 1), lambda i, d=d: ((i[0] // 4) * 4 + ((i[0] % 4) ^ d), i[1])) for d in (1, 2, 3)]
    )
    left = jnp.stack(
        [pick(left, y, 1)]
        + [permute(pick(left, y ^ d, 1), lambda i, d=d: (((i[0] // 4) ^ d) * 4 + i[0] % 4, i[1])) for d in (1, 2, 3)]
    )

    def over_z(value, step):
        def to(i):
            mask = (1, 3)[(step + i[1] % 2) % 2]
            return i[0], ((i[1] // 2) ^ mask) * 2 + i[1] % 2

        return permute(value, to)

    near = over_z(left, 0)
    held = jnp.stack([left, near])
    far = over_z(held, 1)
    one = jnp.where(core == 0, held[1], far[0])
    three = jnp.where(core == 0, far[0], held[1])
    left = jnp.stack([left, one, far[1], three]).reshape(4, 16, 8, 16, 128)
    own = turn(left)
    other = permute(own, lambda d: (d[0], d[1] ^ 1))

    weights = (final_matrix / 1024).astype(jnp.bfloat16).reshape(32, 32, 128)
    weights = jnp.transpose(weights, (2, 1, 0))
    core_index = core.astype(jnp.int32).reshape(1)
    acc = None
    at = 0
    for n, depth in enumerate(STREAMS):
        pieces = []
        for part in range(2):
            e0 = at + part * (depth // 2)
            have = right[e0 : e0 + depth // 2][None]
            for step in range(4):
                got = permute(have, functools.partial(hop, part, step))
                if step < 3:
                    have = jnp.concatenate([have, got], axis=0)
            pieces += [have, got]
        last = n == len(STREAMS) - 1
        acc = product(
            depth,
            core_index,
            own,
            other,
            pieces,
            weights[:, at : at + depth].reshape(128, depth * 32),
            acc,
            pairwise_features if last else None,
            final_offset.reshape(1, 128) if last else None,
        )
        at += depth
    return acc


def solution(mesh):
    placed = (
        P(("row", "col"), None, None),
        P(),
        P(),
        P(),
        P(),
        P(),
        P(),
        P(),
        P(),
        P("row", "col", None),
    )
    return jax.shard_map(
        per_device, mesh=mesh, in_specs=placed, out_specs=P("row", "col", None), check_vma=False
    )
```

time: 454 us -> 133 us (0.29)
  waiting for transfers between devices: 254 us -> 36.1 us
  local copies, waits for them, and re-layouts: 76.8 us -> 10.9 us
  matrix products: 46.2 us -> 0 us
  blocking collectives: 42.6 us -> 0 us
  starting transfers between devices: 0.04 us -> 42.3 us
  Pallas kernels: 0 us -> 37.7 us
  other arithmetic: 19.1 us -> 4.71 us
  between operations: 13.6 us -> 0.49 us
    all_gather x2 -> x0, waiting for transfers between devices: 254 us -> none  [the longest x1 192 us: per_device(): right_tile = lax.all_gather(right_moved, 'row', axis=1, tiled=True)]
    dot_general x10 -> x0, matrix products: 46.2 us -> none  [the longest x4 32.9 us: one_block(): jnp.einsum('sic,sje->ijce', left_piece, right_tile, preferred_element_typ...]
    all_to_all x2 -> x0, blocking collectives: 42.6 us -> none  [the longest x1 24.7 us: per_device(): lax.all_to_all(left, ('row', 'col'), split_axis=1, concat_axis=0, tiled=T...]
    ppermute x0 -> x29, starting transfers between devices: none -> 42.3 us  [permute(): return lax.ppermute(value, ('row', 'col'), pairs)]
    pallas_call x0 -> x4, Pallas kernels: none -> 37.7 us  [the longest x2 29.6 us: product(): pl.pallas_call(functools.partial(product_kernel, depth, acc is None, last...]
    ppermute x0 -> x29, waiting for transfers between devices: none -> 36.1 us  [permute(): return lax.ppermute(value, ('row', 'col'), pairs)]
    while x1 -> x0, local copies, waits for them, and re-layouts: 30.8 us -> none  [per_device(): result = lax.map(one_block, (left_blocks, pair_blocks))]
    reshape x2 -> x3, local copies, waits for them, and re-layouts: 19.2 us -> 0.97 us  [the longest x1 0.74 us: project(): second_offset.reshape(32, 1)]
  transfers between devices with their start and end apart: 2 -> 29, of which waited for: 2 -> 17; matrix products, arithmetic and copies ran while one was open for 6% -> 5% of each run, Pallas kernels for 0% -> 11%
where the time goes in v1:
time: 133 us; the launch traced here: 132 us
  starting transfers between devices  42.3 us (32%)
  Pallas kernels  37.7 us (28%)
  waiting for transfers between devices  36.1 us (27%)
  local copies, waits for them, and re-layouts  10.9 us (8%)
  other arithmetic  4.71 us (4%)
    ppermute x29, starting transfers between devices, permute(): return lax.ppermute(value, ('row', 'col'), pairs)  42.3 us
    ppermute x29, waiting for transfers between devices, permute(): return lax.ppermute(value, ('row', 'col'), pairs)  36.1 us
    pallas_call x2, Pallas kernels, product(): pl.pallas_call(functools.partial(product_kernel, depth, acc is None, last...  29.6 us
    pallas_call x1, Pallas kernels, project(): pl.pallas_call(project_kernel, grid=(8,), in_specs=[pl.BlockSpec((1, 1024...  6.76 us
    unnamed x16, local copies, waits for them, and re-layouts  6.23 us
    concatenate x12, other arithmetic, per_device(): have = jnp.concatenate([have, got], axis=0)  3.66 us
  transfers between devices with their start and end apart: 29, of which 17 were waited for; matrix products, arithmetic and copies ran while one was open for 5% of the time, Pallas kernels for 11%

profile of v1, /device:TPU:0, one launch (start us, length us, event | category | flops | bytes accessed | tf_op | source)
XLA Modules:
  0.0 132.1 jit_solution(2093381549848877164)
XLA Ops:
  2.3 2.2 %copy-done.1 = bf16[8,1024,256]{2,1,0:T(8,128)(2,1)S(1)} copy-done((bf16[8,1024,256]{2,1,0:T(8,128)(2,1)S(1)}, bf16[8,1024,256]{2,1,0:T(8,128)(2,1)}, u32[]{:S(2)}) %copy-start.1) | copy-done | bytes 4194328
  6.6 6.8 %project.1 = bf16[2,256,8,128]{3,2,1,0:T(8,128)(2,1)S(1)} custom-call(bf16[8,1024,256]{2,1,0:T(8,128)(2,1)S(1)} %copy-done.1, f32[1,256]{1,0:T(1,128)S(1)} %bitcast.70, f32[1,256]{1,0:T(1,128)S(1)} %bitcast.71, bf16[256,128]{1,0:T(8,128)(2,1)S(1)} %copy.18.weights_ref, f32[1,128]{1,0:T(1,128)S(1)} %reshape_tile.3.bias_ref, bf16[32,256]{1,0:T(8,128)(2,1)S(1)} %bitcast.69, ...), custom_call_target="tpu_custom_call" | custom-call | tf_op jit(solution)/shard_map/project/pallas_call | solution.py:48
  17.7 2.7 %collective-permute-start.2 = (bf16[4,8,16,128]{3,2,1,0:T(8,128)(2,1)S(1)}, bf16[4,8,16,128]{3,2,1,0:T(8,128)(2,1)S(1)}, u32[]{:S(2)}, u32[]{:S(2)}) collective-permute-start(bf16[4,8,16,128]{3,2,1,0:T(8,128)(2,1)S(1)} %get-tuple-element.27), channel_id=1, source_target_pairs={{0,16},{1,17},{2,18},{3,19},{4,20},{5,21},{6,22},{7,23},{8,24},{9,... | collective-permute-start | bytes 393224 | tf_op jit(solution)/shard_map/ppermute | solution.py:226
  22.2 4.7 %collective-permute-done.2 = bf16[4,8,16,128]{3,2,1,0:T(8,128)(2,1)S(1)} collective-permute-done((bf16[4,8,16,128]{3,2,1,0:T(8,128)(2,1)S(1)}, bf16[4,8,16,128]{3,2,1,0:T(8,128)(2,1)S(1)}, u32[]{:S(2)}, u32[]{:S(2)}) %collective-permute-start.2) | collective-permute-done | bytes 131104 | tf_op jit(solution)/shard_map/ppermute | solution.py:226
  26.9 2.2 %collective-permute-done.3 = bf16[4,8,16,128]{3,2,1,0:T(8,128)(2,1)S(1)} collective-permute-done((bf16[4,8,16,128]{3,2,1,0:T(8,128)(2,1)S(1)}, bf16[4,8,16,128]{3,2,1,0:T(8,128)(2,1)S(1)}, u32[]{:S(2)}, u32[]{:S(2)}) %collective-permute-start.3) | collective-permute-done | bytes 131104 | tf_op jit(solution)/shard_map/ppermute | solution.py:226
  30.9 2.9 %collective-permute-start.5 = (bf16[4,8,16,128]{3,2,1,0:T(8,128)(2,1)S(1)}, bf16[4,8,16,128]{3,2,1,0:T(8,128)(2,1)S(1)}, u32[]{:S(2)}, u32[]{:S(2)}) collective-permute-start(bf16[4,8,16,128]{3,2,1,0:T(8,128)(2,1)S(1)} %get-tuple-element.23), channel_id=1, source_target_pairs={{0,64},{1,65},{2,66},{3,67},{4,68},{5,69},{6,70},{7,71},{8,72},{9,... | collective-permute-start | bytes 393224 | tf_op jit(solution)/shard_map/ppermute | solution.py:226
  34.9 4.7 %collective-permute-done.5 = bf16[4,8,16,128]{3,2,1,0:T(8,128)(2,1)S(1)} collective-permute-done((bf16[4,8,16,128]{3,2,1,0:T(8,128)(2,1)S(1)}, bf16[4,8,16,128]{3,2,1,0:T(8,128)(2,1)S(1)}, u32[]{:S(2)}, u32[]{:S(2)}) %collective-permute-start.5) | collective-permute-done | bytes 131104 | tf_op jit(solution)/shard_map/ppermute | solution.py:226
  41.5 2.0 %collective-permute-start.7 = (bf16[4,4,8,16,128]{4,3,2,1,0:T(8,128)(2,1)S(1)}, bf16[4,4,8,16,128]{4,3,2,1,0:T(8,128)(2,1)S(1)}, u32[]{:S(2)}, u32[]{:S(2)}) collective-permute-start(bf16[4,4,8,16,128]{4,3,2,1,0:T(8,128)(2,1)S(1)} %get-tuple-element.20), channel_id=1, source_target_pairs={{0,2},{1,7},{2,0},{3,5},{4,6},{5,3},{6,4},{7,1},{8,10},{9,15},{10,... | collective-permute-start | bytes 1572872 | tf_op jit(solution)/shard_map/ppermute | solution.py:226
  43.8 3.9 %collective-permute-start.11 = (bf16[32,16,128]{2,1,0:T(8,128)(2,1)S(1)}, bf16[32,16,128]{2,1,0:T(8,128)(2,1)S(1)}, u32[]{:S(2)}, u32[]{:S(2)}) collective-permute-start(bf16[32,16,128]{2,1,0:T(8,128)(2,1)S(1)} %get-tuple-element.17), channel_id=1, source_target_pairs={{0,4},{1,5},{2,6},{3,7},{4,0},{5,1},{6,2},{7,3},{8,12},{9,13},{10,... | collective-permute-start | bytes 393224 | tf_op jit(solution)/shard_map/ppermute | solution.py:226
  48.4 5.3 %collective-permute-done.7 = bf16[4,4,8,16,128]{4,3,2,1,0:T(8,128)(2,1)S(1)} collective-permute-done((bf16[4,4,8,16,128]{4,3,2,1,0:T(8,128)(2,1)S(1)}, bf16[4,4,8,16,128]{4,3,2,1,0:T(8,128)(2,1)S(1)}, u32[]{:S(2)}, u32[]{:S(2)}) %collective-permute-start.7) | collective-permute-done | bytes 524320 | tf_op jit(solution)/shard_map/ppermute | solution.py:226
  53.7 2.7 %collective-permute-start.8 = (bf16[2,4,4,8,16,128]{5,4,3,2,1,0:T(8,128)(2,1)S(1)}, bf16[2,4,4,8,16,128]{5,4,3,2,1,0:T(8,128)(2,1)S(1)}, u32[]{:S(2)}, u32[]{:S(2)}) collective-permute-start(bf16[2,4,4,8,16,128]{5,4,3,2,1,0:T(8,128)(2,1)S(1)} %pad_maximum_fusion.1), channel_id=1, source_target_pairs={{0,6},{1,3},{2,4},{3,1},{4,2},{5,7},{6,0},{7,5},{8,14},{9,11},{10,... | collective-permute-start | bytes 3145736 | tf_op jit(solution)/shard_map/ppermute | solution.py:226
  56.4 2.1 %collective-permute-done.11 = bf16[32,16,128]{2,1,0:T(8,128)(2,1)S(1)} collective-permute-done((bf16[32,16,128]{2,1,0:T(8,128)(2,1)S(1)}, bf16[32,16,128]{2,1,0:T(8,128)(2,1)S(1)}, u32[]{:S(2)}, u32[]{:S(2)}) %collective-permute-start.11) | collective-permute-done | bytes 131104 | tf_op jit(solution)/shard_map/ppermute | solution.py:226
  58.8 1.9 %collective-permute-start.17 = (bf16[1,8,64,128]{3,2,1,0:T(8,128)(2,1)S(1)}, bf16[1,8,64,128]{3,2,1,0:T(8,128)(2,1)S(1)}, u32[]{:S(2)}, u32[]{:S(2)}) collective-permute-start(bf16[1,8,64,128]{3,2,1,0:T(8,128)(2,1)S(1)} %get-tuple-element.13), channel_id=1, source_target_pairs={{0,32},{1,97},{2,34},{3,99},{4,36},{5,101},{6,38},{7,103},{8,40},{... | collective-permute-start | bytes 393224 | tf_op jit(solution)/shard_map/ppermute | solution.py:226
  60.7 2.0 %collective-permute-start.13 = (bf16[1,8,64,128]{3,2,1,0:T(8,128)(2,1)S(1)}, bf16[1,8,64,128]{3,2,1,0:T(8,128)(2,1)S(1)}, u32[]{:S(2)}, u32[]{:S(2)}) collective-permute-start(bf16[1,8,64,128]{3,2,1,0:T(8,128)(2,1)S(1)} %get-tuple-element.14), channel_id=1, source_target_pairs={{0,8},{1,25},{2,10},{3,27},{4,12},{5,29},{6,14},{7,31},{8,0},{9,17... | collective-permute-start | bytes 393224 | tf_op jit(solution)/shard_map/ppermute | solution.py:226
  65.6 2.3 %collective-permute-start.18 = (bf16[2,8,64,128]{3,2,1,0:T(8,128)(2,1)S(1)}, bf16[2,8,64,128]{3,2,1,0:T(8,128)(2,1)S(1)}, u32[]{:S(2)}, u32[]{:S(2)}) collective-permute-start(bf16[2,8,64,128]{3,2,1,0:T(8,128)(2,1)S(1)} %pad_maximum_fusion.14), channel_id=1, source_target_pairs={{0,96},{1,33},{2,98},{3,35},{4,100},{5,37},{6,102},{7,39},{8,104},... | collective-permute-start | bytes 786440 | tf_op jit(solution)/shard_map/ppermute | solution.py:226
  67.9 2.6 %collective-permute-start.14 = (bf16[2,8,64,128]{3,2,1,0:T(8,128)(2,1)S(1)}, bf16[2,8,64,128]{3,2,1,0:T(8,128)(2,1)S(1)}, u32[]{:S(2)}, u32[]{:S(2)}) collective-permute-start(bf16[2,8,64,128]{3,2,1,0:T(8,128)(2,1)S(1)} %pad_maximum_fusion.13), channel_id=1, source_target_pairs={{0,24},{1,9},{2,26},{3,11},{4,28},{5,13},{6,30},{7,15},{8,16},{9,1... | collective-permute-start | bytes 786440 | tf_op jit(solution)/shard_map/ppermute | solution.py:226
  75.7 2.8 %collective-permute-done.14 = bf16[2,8,64,128]{3,2,1,0:T(8,128)(2,1)S(1)} collective-permute-done((bf16[2,8,64,128]{3,2,1,0:T(8,128)(2,1)S(1)}, bf16[2,8,64,128]{3,2,1,0:T(8,128)(2,1)S(1)}, u32[]{:S(2)}, u32[]{:S(2)}) %collective-permute-start.14) | collective-permute-done | bytes 262176 | tf_op jit(solution)/shard_map/ppermute | solution.py:226
  83.7 3.1 %collective-permute-start.24 = (bf16[8,8,64,128]{3,2,1,0:T(8,128)(2,1)}, bf16[8,8,64,128]{3,2,1,0:T(8,128)(2,1)}, u32[]{:S(2)}, u32[]{:S(2)}) collective-permute-start(bf16[8,8,64,128]{3,2,1,0:T(8,128)(2,1)} %pad_maximum_fusion.4.a_lo), channel_id=1, source_target_pairs={{0,96},{1,33},{2,98},{3,35},{4,100},{5,37},{6,102},{7,39},{8,104},... | collective-permute-start | bytes 3145736 | tf_op jit(solution)/shard_map/ppermute | solution.py:226
  86.9 2.1 %collective-permute-done.19 = bf16[4,8,64,128]{3,2,1,0:T(8,128)(2,1)S(1)} collective-permute-done((bf16[4,8,64,128]{3,2,1,0:T(8,128)(2,1)S(1)}, bf16[4,8,64,128]{3,2,1,0:T(8,128)(2,1)S(1)}, u32[]{:S(2)}, u32[]{:S(2)}) %collective-permute-start.19) | collective-permute-done | bytes 524320 | tf_op jit(solution)/shard_map/ppermute | solution.py:226
  91.9 4.0 %collective-permute-start.16 = (bf16[8,8,64,128]{3,2,1,0:T(8,128)(2,1)}, bf16[8,8,64,128]{3,2,1,0:T(8,128)(2,1)}, u32[]{:S(2)}, u32[]{:S(2)}) collective-permute-start(bf16[8,8,64,128]{3,2,1,0:T(8,128)(2,1)} %pad_maximum_fusion.2.a_lo), channel_id=1, source_target_pairs={{0,96},{1,33},{2,98},{3,35},{4,100},{5,37},{6,102},{7,39},{8,104},... | collective-permute-start | bytes 3145736 | tf_op jit(solution)/shard_map/ppermute | solution.py:226
  97.8 2.6 %collective-permute-done.24.a_hi = bf16[8,8,64,128]{3,2,1,0:T(8,128)(2,1)} collective-permute-done((bf16[8,8,64,128]{3,2,1,0:T(8,128)(2,1)}, bf16[8,8,64,128]{3,2,1,0:T(8,128)(2,1)}, u32[]{:S(2)}, u32[]{:S(2)}) %collective-permute-start.24) | collective-permute-done | bytes 1048608 | tf_op jit(solution)/shard_map/ppermute | solution.py:226
  100.4 13.6 %product.2.refs_0_ = f32[64,128,128]{2,1,0:T(8,128)S(1)} custom-call(s32[1]{0:T(128)} %bitcast.core_ref, bf16[1024,1024]{1,0:T(8,128)(2,1)S(1)} %turn.1.own_ref, bf16[1024,1024]{1,0:T(8,128)(2,1)} %collective-permute-done.9.other_ref, bf16[8,8,64,128]{3,2,1,0:T(8,128)(2,1)} %pad_maximum_fusion.4.a_lo, bf16[8,8,64,128]{3,2,1,0:T(8,128)(2,1)} %collective-permute-done.24.a_hi, ...), custom_call_target="tpu_custom_call" | custom-call | tf_op jit(solution)/shard_map/product/pallas_call | solution.py:191
  114.0 2.0 %copy-done = f32[64,128,128]{2,1,0:T(8,128)} copy-done((f32[64,128,128]{2,1,0:T(8,128)}, f32[64,128,128]{2,1,0:T(8,128)S(1)}, u32[]{:S(2)}) %copy-start) | copy-done | bytes 4194328
  116.0 16.0 %product.3 = bf16[64,128,128]{2,1,0:T(8,128)(2,1)} custom-call(s32[1]{0:T(128)} %bitcast.core_ref, bf16[1024,1024]{1,0:T(8,128)(2,1)S(1)} %turn.1.own_ref, bf16[1024,1024]{1,0:T(8,128)(2,1)} %collective-permute-done.9.other_ref, bf16[8,8,64,128]{3,2,1,0:T(8,128)(2,1)} %pad_maximum_fusion.2.a_lo, bf16[8,8,64,128]{3,2,1,0:T(8,128)(2,1)} %collective-permute-done.16.a_hi, ...), custom_call_target="tpu_custom_call" | custom-call | tf_op jit(solution)/shard_map/product/pallas_call | solution.py:191
  (91 shorter events, 34.5 us)
Async XLA Ops:
  17.7 9.2 %collective-permute-start.2 = (bf16[4,8,16,128]{3,2,1,0:T(8,128)(2,1)S(1)}, bf16[4,8,16,128]{3,2,1,0:T(8,128)(2,1)S(1)}, u32[]{:S(2)}, u32[]{:S(2)}) collective-permute-start(bf16[4,8,16,128]{3,2,1,0:T(8,128)(2,1)S(1)} %get-tuple-element.27), channel_id=1, source_target_pairs={{0,16},{1,17},{2,18},{3,19},{4,20},{5,21},{6,22},{7,23},{8,24},{9,... | collective-permute-start | bytes 393224 | tf_op jit(solution)/shard_map/ppermute | solution.py:226
  20.4 8.7 %collective-permute-start.3 = (bf16[4,8,16,128]{3,2,1,0:T(8,128)(2,1)S(1)}, bf16[4,8,16,128]{3,2,1,0:T(8,128)(2,1)S(1)}, u32[]{:S(2)}, u32[]{:S(2)}) collective-permute-start(bf16[4,8,16,128]{3,2,1,0:T(8,128)(2,1)S(1)} %get-tuple-element.26), channel_id=1, source_target_pairs={{0,24},{1,25},{2,26},{3,27},{4,28},{5,29},{6,30},{7,31},{8,16},{9,... | collective-permute-start | bytes 393224 | tf_op jit(solution)/shard_map/ppermute | solution.py:226
  30.9 8.7 %collective-permute-start.5 = (bf16[4,8,16,128]{3,2,1,0:T(8,128)(2,1)S(1)}, bf16[4,8,16,128]{3,2,1,0:T(8,128)(2,1)S(1)}, u32[]{:S(2)}, u32[]{:S(2)}) collective-permute-start(bf16[4,8,16,128]{3,2,1,0:T(8,128)(2,1)S(1)} %get-tuple-element.23), channel_id=1, source_target_pairs={{0,64},{1,65},{2,66},{3,67},{4,68},{5,69},{6,70},{7,71},{8,72},{9,... | collective-permute-start | bytes 393224 | tf_op jit(solution)/shard_map/ppermute | solution.py:226
  33.8 7.7 %collective-permute-start.6 = (bf16[4,8,16,128]{3,2,1,0:T(8,128)(2,1)S(1)}, bf16[4,8,16,128]{3,2,1,0:T(8,128)(2,1)S(1)}, u32[]{:S(2)}, u32[]{:S(2)}) collective-permute-start(bf16[4,8,16,128]{3,2,1,0:T(8,128)(2,1)S(1)} %get-tuple-element.22), channel_id=1, source_target_pairs={{0,96},{1,97},{2,98},{3,99},{4,100},{5,101},{6,102},{7,103},{8,104... | collective-permute-start | bytes 393224 | tf_op jit(solution)/shard_map/ppermute | solution.py:226
  41.5 12.1 %collective-permute-start.7 = (bf16[4,4,8,16,128]{4,3,2,1,0:T(8,128)(2,1)S(1)}, bf16[4,4,8,16,128]{4,3,2,1,0:T(8,128)(2,1)S(1)}, u32[]{:S(2)}, u32[]{:S(2)}) collective-permute-start(bf16[4,4,8,16,128]{4,3,2,1,0:T(8,128)(2,1)S(1)} %get-tuple-element.20), channel_id=1, source_target_pairs={{0,2},{1,7},{2,0},{3,5},{4,6},{5,3},{6,4},{7,1},{8,10},{9,15},{10,... | collective-permute-start | bytes 1572872 | tf_op jit(solution)/shard_map/ppermute | solution.py:226
  43.6 12.9 %collective-permute-start.10 = (bf16[32,16,128]{2,1,0:T(8,128)(2,1)S(1)}, bf16[32,16,128]{2,1,0:T(8,128)(2,1)S(1)}, u32[]{:S(2)}, u32[]{:S(2)}) collective-permute-start(bf16[32,16,128]{2,1,0:T(8,128)(2,1)S(1)} %get-tuple-element.18), channel_id=1, source_target_pairs={{0,2},{1,3},{2,0},{3,1},{4,6},{5,7},{6,4},{7,5},{8,10},{9,11},{10,... | collective-permute-start | bytes 393224 | tf_op jit(solution)/shard_map/ppermute | solution.py:226
  43.8 14.7 %collective-permute-start.11 = (bf16[32,16,128]{2,1,0:T(8,128)(2,1)S(1)}, bf16[32,16,128]{2,1,0:T(8,128)(2,1)S(1)}, u32[]{:S(2)}, u32[]{:S(2)}) collective-permute-start(bf16[32,16,128]{2,1,0:T(8,128)(2,1)S(1)} %get-tuple-element.17), channel_id=1, source_target_pairs={{0,4},{1,5},{2,6},{3,7},{4,0},{5,1},{6,2},{7,3},{8,12},{9,13},{10,... | collective-permute-start | bytes 393224 | tf_op jit(solution)/shard_map/ppermute | solution.py:226
  47.6 10.9 %collective-permute-start.12 = (bf16[32,16,128]{2,1,0:T(8,128)(2,1)S(1)}, bf16[32,16,128]{2,1,0:T(8,128)(2,1)S(1)}, u32[]{:S(2)}, u32[]{:S(2)}) collective-permute-start(bf16[32,16,128]{2,1,0:T(8,128)(2,1)S(1)} %get-tuple-element.16), channel_id=1, source_target_pairs={{0,6},{1,7},{2,4},{3,5},{4,2},{5,3},{6,0},{7,1},{8,14},{9,15},{10,... | collective-permute-start | bytes 393224 | tf_op jit(solution)/shard_map/ppermute | solution.py:226
  53.7 17.8 %collective-permute-start.8 = (bf16[2,4,4,8,16,128]{5,4,3,2,1,0:T(8,128)(2,1)S(1)}, bf16[2,4,4,8,16,128]{5,4,3,2,1,0:T(8,128)(2,1)S(1)}, u32[]{:S(2)}, u32[]{:S(2)}) collective-permute-start(bf16[2,4,4,8,16,128]{5,4,3,2,1,0:T(8,128)(2,1)S(1)} %pad_maximum_fusion.1), channel_id=1, source_target_pairs={{0,6},{1,3},{2,4},{3,1},{4,2},{5,7},{6,0},{7,5},{8,14},{9,11},{10,... | collective-permute-start | bytes 3145736 | tf_op jit(solution)/shard_map/ppermute | solution.py:226
  58.8 6.8 %collective-permute-start.17 = (bf16[1,8,64,128]{3,2,1,0:T(8,128)(2,1)S(1)}, bf16[1,8,64,128]{3,2,1,0:T(8,128)(2,1)S(1)}, u32[]{:S(2)}, u32[]{:S(2)}) collective-permute-start(bf16[1,8,64,128]{3,2,1,0:T(8,128)(2,1)S(1)} %get-tuple-element.13), channel_id=1, source_target_pairs={{0,32},{1,97},{2,34},{3,99},{4,36},{5,101},{6,38},{7,103},{8,40},{... | collective-permute-start | bytes 393224 | tf_op jit(solution)/shard_map/ppermute | solution.py:226
  60.7 7.2 %collective-permute-start.13 = (bf16[1,8,64,128]{3,2,1,0:T(8,128)(2,1)S(1)}, bf16[1,8,64,128]{3,2,1,0:T(8,128)(2,1)S(1)}, u32[]{:S(2)}, u32[]{:S(2)}) collective-permute-start(bf16[1,8,64,128]{3,2,1,0:T(8,128)(2,1)S(1)} %get-tuple-element.14), channel_id=1, source_target_pairs={{0,8},{1,25},{2,10},{3,27},{4,12},{5,29},{6,14},{7,31},{8,0},{9,17... | collective-permute-start | bytes 393224 | tf_op jit(solution)/shard_map/ppermute | solution.py:226
  63.7 7.7 %collective-permute-start.26 = (bf16[2,8,64,128]{3,2,1,0:T(8,128)(2,1)S(1)}, bf16[2,8,64,128]{3,2,1,0:T(8,128)(2,1)S(1)}, u32[]{:S(2)}, u32[]{:S(2)}) collective-permute-start(bf16[2,8,64,128]{3,2,1,0:T(8,128)(2,1)S(1)} %pad_maximum_fusion.16), channel_id=1, source_target_pairs={{0,96},{1,33},{2,98},{3,35},{4,100},{5,37},{6,102},{7,39},{8,104},... | collective-permute-start | bytes 786440 | tf_op jit(solution)/shard_map/ppermute | solution.py:226
  64.7 8.6 %collective-permute-start.22 = (bf16[2,8,64,128]{3,2,1,0:T(8,128)(2,1)S(1)}, bf16[2,8,64,128]{3,2,1,0:T(8,128)(2,1)S(1)}, u32[]{:S(2)}, u32[]{:S(2)}) collective-permute-start(bf16[2,8,64,128]{3,2,1,0:T(8,128)(2,1)S(1)} %pad_maximum_fusion.15), channel_id=1, source_target_pairs={{0,24},{1,9},{2,26},{3,11},{4,28},{5,13},{6,30},{7,15},{8,16},{9,1... | collective-permute-start | bytes 786440 | tf_op jit(solution)/shard_map/ppermute | solution.py:226
  65.6 8.7 %collective-permute-start.18 = (bf16[2,8,64,128]{3,2,1,0:T(8,128)(2,1)S(1)}, bf16[2,8,64,128]{3,2,1,0:T(8,128)(2,1)S(1)}, u32[]{:S(2)}, u32[]{:S(2)}) collective-permute-start(bf16[2,8,64,128]{3,2,1,0:T(8,128)(2,1)S(1)} %pad_maximum_fusion.14), channel_id=1, source_target_pairs={{0,96},{1,33},{2,98},{3,35},{4,100},{5,37},{6,102},{7,39},{8,104},... | collective-permute-start | bytes 786440 | tf_op jit(solution)/shard_map/ppermute | solution.py:226
  67.9 10.5 %collective-permute-start.14 = (bf16[2,8,64,128]{3,2,1,0:T(8,128)(2,1)S(1)}, bf16[2,8,64,128]{3,2,1,0:T(8,128)(2,1)S(1)}, u32[]{:S(2)}, u32[]{:S(2)}) collective-permute-start(bf16[2,8,64,128]{3,2,1,0:T(8,128)(2,1)S(1)} %pad_maximum_fusion.13), channel_id=1, source_target_pairs={{0,24},{1,9},{2,26},{3,11},{4,28},{5,13},{6,30},{7,15},{8,16},{9,1... | collective-permute-start | bytes 786440 | tf_op jit(solution)/shard_map/ppermute | solution.py:226
  71.4 9.3 %collective-permute-start.27 = (bf16[4,8,64,128]{3,2,1,0:T(8,128)(2,1)S(1)}, bf16[4,8,64,128]{3,2,1,0:T(8,128)(2,1)S(1)}, u32[]{:S(2)}, u32[]{:S(2)}) collective-permute-start(bf16[4,8,64,128]{3,2,1,0:T(8,128)(2,1)S(1)} %pad_maximum_fusion.12), channel_id=1, source_target_pairs={{0,8},{1,25},{2,10},{3,27},{4,12},{5,29},{6,14},{7,31},{8,0},{9,17... | collective-permute-start | bytes 1572872 | tf_op jit(solution)/shard_map/ppermute | solution.py:226
  73.2 27.1 %collective-permute-start.9 = (bf16[1024,1024]{1,0:T(8,128)(2,1)S(1)}, bf16[1024,1024]{1,0:T(8,128)(2,1)}, u32[]{:S(2)}, u32[]{:S(2)}) collective-permute-start(bf16[1024,1024]{1,0:T(8,128)(2,1)S(1)} %turn.1.own_ref), channel_id=1, source_target_pairs={{0,1},{1,0},{2,3},{3,2},{4,5},{5,4},{6,7},{7,6},{8,9},{9,8},{10,11... | collective-permute-start | bytes 6291464 | tf_op jit(solution)/shard_map/ppermute | solution.py:226
  73.4 9.3 %collective-permute-start.23 = (bf16[4,8,64,128]{3,2,1,0:T(8,128)(2,1)S(1)}, bf16[4,8,64,128]{3,2,1,0:T(8,128)(2,1)S(1)}, u32[]{:S(2)}, u32[]{:S(2)}) collective-permute-start(bf16[4,8,64,128]{3,2,1,0:T(8,128)(2,1)S(1)} %pad_maximum_fusion.11), channel_id=1, source_target_pairs={{0,32},{1,97},{2,34},{3,99},{4,36},{5,101},{6,38},{7,103},{8,40},{... | collective-permute-start | bytes 1572872 | tf_op jit(solution)/shard_map/ppermute | solution.py:226
  74.3 14.7 %collective-permute-start.19 = (bf16[4,8,64,128]{3,2,1,0:T(8,128)(2,1)S(1)}, bf16[4,8,64,128]{3,2,1,0:T(8,128)(2,1)S(1)}, u32[]{:S(2)}, u32[]{:S(2)}) collective-permute-start(bf16[4,8,64,128]{3,2,1,0:T(8,128)(2,1)S(1)} %pad_maximum_fusion.10), channel_id=1, source_target_pairs={{0,8},{1,25},{2,10},{3,27},{4,12},{5,29},{6,14},{7,31},{8,0},{9,17... | collective-permute-start | bytes 1572872 | tf_op jit(solution)/shard_map/ppermute | solution.py:226
  78.5 12.2 %collective-permute-start.15 = (bf16[4,8,64,128]{3,2,1,0:T(8,128)(2,1)S(1)}, bf16[4,8,64,128]{3,2,1,0:T(8,128)(2,1)S(1)}, u32[]{:S(2)}, u32[]{:S(2)}) collective-permute-start(bf16[4,8,64,128]{3,2,1,0:T(8,128)(2,1)S(1)} %pad_maximum_fusion.9), channel_id=1, source_target_pairs={{0,32},{1,97},{2,34},{3,99},{4,36},{5,101},{6,38},{7,103},{8,40},{... | collective-permute-start | bytes 1572872 | tf_op jit(solution)/shard_map/ppermute | solution.py:226
  80.8 17.0 %collective-permute-start.28 = (bf16[8,8,64,128]{3,2,1,0:T(8,128)(2,1)S(1)}, bf16[8,8,64,128]{3,2,1,0:T(8,128)(2,1)}, u32[]{:S(2)}, u32[]{:S(2)}) collective-permute-start(bf16[8,8,64,128]{3,2,1,0:T(8,128)(2,1)S(1)} %pad_maximum_fusion.5.b_lo), channel_id=1, source_target_pairs={{0,24},{1,9},{2,26},{3,11},{4,28},{5,13},{6,30},{7,15},{8,16},{9,1... | collective-permute-start | bytes 3145736 | tf_op jit(solution)/shard_map/ppermute | solution.py:226
  83.7 16.6 %collective-permute-start.24 = (bf16[8,8,64,128]{3,2,1,0:T(8,128)(2,1)}, bf16[8,8,64,128]{3,2,1,0:T(8,128)(2,1)}, u32[]{:S(2)}, u32[]{:S(2)}) collective-permute-start(bf16[8,8,64,128]{3,2,1,0:T(8,128)(2,1)} %pad_maximum_fusion.4.a_lo), channel_id=1, source_target_pairs={{0,96},{1,33},{2,98},{3,35},{4,100},{5,37},{6,102},{7,39},{8,104},... | collective-permute-start | bytes 3145736 | tf_op jit(solution)/shard_map/ppermute | solution.py:226
  90.1 25.9 %collective-permute-start.20 = (bf16[8,8,64,128]{3,2,1,0:T(8,128)(2,1)}, bf16[8,8,64,128]{3,2,1,0:T(8,128)(2,1)}, u32[]{:S(2)}, u32[]{:S(2)}) collective-permute-start(bf16[8,8,64,128]{3,2,1,0:T(8,128)(2,1)} %pad_maximum_fusion.3.b_lo), channel_id=1, source_target_pairs={{0,24},{1,9},{2,26},{3,11},{4,28},{5,13},{6,30},{7,15},{8,16},{9,1... | collective-permute-start | bytes 3145736 | tf_op jit(solution)/shard_map/ppermute | solution.py:226
  91.9 24.1 %collective-permute-start.16 = (bf16[8,8,64,128]{3,2,1,0:T(8,128)(2,1)}, bf16[8,8,64,128]{3,2,1,0:T(8,128)(2,1)}, u32[]{:S(2)}, u32[]{:S(2)}) collective-permute-start(bf16[8,8,64,128]{3,2,1,0:T(8,128)(2,1)} %pad_maximum_fusion.2.a_lo), channel_id=1, source_target_pairs={{0,96},{1,33},{2,98},{3,35},{4,100},{5,37},{6,102},{7,39},{8,104},... | collective-permute-start | bytes 3145736 | tf_op jit(solution)/shard_map/ppermute | solution.py:226
  (13 other events, 74.4 us)

commit v2 on v0

v2 whole, which is shorter than its diff:
```python
import functools

import jax
import jax.numpy as jnp
import numpy as np
from jax import lax
from jax.experimental import pallas as pl
from jax.experimental.pallas import tpu as pltpu
from jax.sharding import PartitionSpec as P

MIB = 2**20
UNITS = [()]
for _step in range(1, 4):
    UNITS += [steps + (_step,) for steps in UNITS]
ORDER = (0,1,2,4,3,5,6,7)
PRODUCTS = ((0,2,(0,0,0,0),8000),(2,5,(2,2,2,2),12000),(5,8,(5,5,5,5),80))


def project_kernel(x_ref, gain_ref, offset_ref, first_ref, first_offset_ref, second_ref, second_offset_ref, out_ref, held, left, right, ready):
    def fetch(s):
        return pltpu.make_async_copy(x_ref.at[s], held.at[s], ready.at[s])

    for s in range(8):
        fetch(s).start()
    zeros = jnp.zeros((32, 256), jnp.bfloat16)
    first = jnp.concatenate(
        [jnp.concatenate([first_ref[...] if a == b else zeros for b in range(4)], axis=1) for a in range(4)], axis=0
    )
    first_offset = jnp.concatenate([first_offset_ref[...]] * 4, axis=1)
    diagonal = lax.broadcasted_iota(jnp.int32, (32, 32), 0) == lax.broadcasted_iota(jnp.int32, (32, 32), 1)
    second_offset = jnp.sum(jnp.where(diagonal, second_offset_ref[...], 0.0), axis=1, keepdims=True)
    contract_last = (((1,), (1,)), ((), ()))

    for s in range(8):
        for t in {0: (0,), 1: (1, 2, 3), 4: (4, 5, 6, 7)}.get(s, ()):
            fetch(t).wait()
        x = held[s].astype(jnp.float32)
        mean = jnp.mean(x, axis=-1, keepdims=True)
        centred = x - mean
        variance = jnp.mean(centred * centred, axis=-1, keepdims=True)
        normed = (centred * lax.rsqrt(variance + 1e-05) * gain_ref[...] + offset_ref[...]).astype(jnp.bfloat16)
        grouped = normed.reshape(16, 4, 16, 256)
        grouped = jnp.concatenate([grouped[:, a].reshape(256, 256) for a in range(4)], axis=1)
        dense = lax.dot_general(grouped, first, contract_last, preferred_element_type=jnp.float32)
        left[pl.ds(s, 256, stride=8), :] = dense + first_offset
        turned = lax.dot_general(second_ref[...], normed, contract_last, preferred_element_type=jnp.float32)
        turned = turned + second_offset
        for c in range(8):
            right[c, pl.ds(s, 32, stride=8), :] = turned[:, c * 128 : (c + 1) * 128]

    for r in range(16):
        rows = left[r * 128 : (r + 1) * 128, :].astype(jnp.bfloat16).reshape(8, 2, 8, 128)
        for d in range(2):
            out_ref[r, :, :, d * 128 : (d + 1) * 128] = rows[:, d]
    for c in range(8):
        rows = right[c].astype(jnp.bfloat16).reshape(16, 2, 8, 128)
        for d in range(2):
            out_ref[:, c, :, 256 + d * 128 : 256 + (d + 1) * 128] = rows[:, d]


def project(x, gain, offset, first, first_offset, second, second_offset):
    whole = pl.BlockSpec(memory_space=pltpu.VMEM)
    return pl.pallas_call(
        project_kernel,
        in_specs=[pl.BlockSpec(memory_space=pl.ANY)] + [whole] * 6,
        out_specs=whole,
        out_shape=jax.ShapeDtypeStruct((16, 8, 8, 512), jnp.bfloat16),
        scratch_shapes=[
            pltpu.VMEM((8, 1024, 256), jnp.bfloat16),
            pltpu.VMEM((2048, 128), jnp.float32),
            pltpu.VMEM((8, 256, 128), jnp.float32),
            pltpu.SemaphoreType.DMA((8,)),
        ],
        compiler_params=pltpu.CompilerParams(vmem_limit_bytes=58 * MIB),
        name="project",
    )(
        x,
        gain.reshape(1, 256),
        offset.reshape(1, 256),
        first.T,
        first_offset.reshape(1, 32),
        second.T,
        second_offset.reshape(1, 32),
    )


def split_kernel(x_ref, left_ref, right_ref):
    for n in range(8):
        at = n * 128
        left_ref[:, at : at + 128] = jnp.transpose(x_ref[at : at + 128, :256])
    for d in range(2):
        right_ref[d] = x_ref[:, 256 + d * 128 : 256 + (d + 1) * 128]


def split(received):
    return pl.pallas_call(
        split_kernel,
        out_shape=(
            jax.ShapeDtypeStruct((256, 1024), jnp.bfloat16),
            jax.ShapeDtypeStruct((2, 1024, 128), jnp.bfloat16),
        ),
        compiler_params=pltpu.CompilerParams(vmem_limit_bytes=16 * MIB),
        name="split",
    )(received)


def product_kernel(low, high, starts, last, place_ref, *refs):
    refs = list(refs)
    blocks = [b for b in range(4) if starts[b] is not None]
    left_refs = {b: (refs.pop(0), refs.pop(0)) for b in blocks}
    right_refs = [refs.pop(0) for _ in range(2 * (high - low))]
    weights_ref = refs.pop(0)
    adds = any(starts[b] for b in blocks)
    acc_ref = refs.pop(0) if adds else None
    pair_ref, offset_ref = (refs.pop(0), refs.pop(0)) if last else (None, None)
    out_ref, left, right, outer, total = refs[:5]
    refs = refs[5:]
    paired, result = (refs.pop(0), refs.pop(0)) if last else (None, None)
    left_sem, right_sem, acc_sem, pair_sem, out_sem = refs
    core = place_ref[4]

    def left_copy(b, theirs):
        rows = pl.multiple_of(b * 512 + jnp.where(core == theirs, 0, 256), 256)
        return pltpu.make_async_copy(left_refs[b][theirs], left.at[pl.ds(rows, 256)], left_sem.at[b, theirs])

    def right_copy(n):
        return pltpu.make_async_copy(right_refs[n], right.at[pl.ds(2 * n, 2)], right_sem.at[n])

    def acc_copy(b):
        return pltpu.make_async_copy(acc_ref.at[b], total.at[b], acc_sem.at[b])

    def tile(b, a):
        return pl.ds(pl.multiple_of(a * 16 + place_ref[b] * 4, 4), 4)

    def pair_copy(b, a):
        return pltpu.make_async_copy(pair_ref.at[tile(b, a)], paired.at[b, a], pair_sem.at[b, a])

    def out_copies(b):
        if last:
            return [pltpu.make_async_copy(result.at[b, a], out_ref.at[tile(b, a)], out_sem.at[b, a]) for a in range(4)]
        return [pltpu.make_async_copy(total.at[b], out_ref.at[b], out_sem.at[b, 0])]

    for b in blocks:
        for theirs in range(2):
            left_copy(b, theirs).start()
        if b == blocks[0]:
            for n in range(len(right_refs)):
                right_copy(n).start()
        if starts[b]:
            acc_copy(b).start()
        if last:
            for a in range(4):
                pair_copy(b, a).start()

    weights = weights_ref[:, low * 128 : high * 128]

    def second(b, first_unit, pairs):
        for at in pairs:
            rows = slice((first_unit - low) * 128, (high - low) * 128)
            both = jnp.dot(weights[:, rows], outer[b % 2, at, rows], preferred_element_type=jnp.float32)
            for d in range(2):
                i = at * 2 + d
                update = both[:, d * 128 : (d + 1) * 128]
                if first_unit:
                    update = update + total[b, i]
                if last:
                    a, t = i % 4, i // 4
                    update = jnp.transpose(update) + offset_ref[...] + paired[b, a, t].astype(jnp.float32)
                    result[b, a, t] = update.astype(result.dtype)
                else:
                    total[b, i] = update

    arrived = 0
    for n, b in enumerate(blocks + [None]):
        before = blocks[n - 1] if n else None
        if n == 0:
            for theirs in range(2):
                left_copy(b, theirs).wait()
        if n == 1:
            for other in blocks:
                if other != blocks[0]:
                    for theirs in range(2):
                        left_copy(other, theirs).wait()
                if starts[other]:
                    acc_copy(other).wait()
                if last:
                    for a in range(4):
                        pair_copy(other, a).wait()
        units = range(starts[b] - low, high - low) if b is not None else range(2)
        for count, unit in enumerate(units):
            if b is not None:
                while arrived <= unit or (count == len(units) - 1 and arrived < high - low):
                    right_copy(2 * arrived).wait()
                    right_copy(2 * arrived + 1).wait()
                    arrived += 1
                channels = jnp.concatenate([right[4 * unit + e] for e in range(4)], axis=1)
                m = jnp.dot(left[b * 512 : (b + 1) * 512, :], channels, preferred_element_type=jnp.float32)
                m = m.astype(jnp.bfloat16)
                for i in range(16):
                    for e in range(4):
                        at = (4 * unit + e) * 32
                        outer[b % 2, i // 2, at : at + 32, (i % 2) * 128 : (i % 2 + 1) * 128] = m[
                            i * 32 : (i + 1) * 32, e * 128 : (e + 1) * 128
                        ]
            if before is not None:
                second(before, starts[before], range(count * 8 // len(units), (count + 1) * 8 // len(units)))
        if before is not None:
            for copy in out_copies(before):
                copy.start()
    for b in blocks:
        for copy in out_copies(b):
            copy.wait()


def product(place, left, right, low, high, starts, cost, weights, acc, pair, offset):
    depth = 4 * (high - low)
    blocks = [b for b in range(4) if starts[b] is not None]
    anywhere = pl.BlockSpec(memory_space=pl.ANY)
    whole = pl.BlockSpec(memory_space=pltpu.VMEM)
    operands = [piece for b in blocks for piece in left[b]] + right
    specs = [anywhere] * len(operands) + [whole]
    operands.append(weights)
    scratch = [
        pltpu.VMEM((2048, 1024), jnp.bfloat16),
        pltpu.VMEM((depth, 1024, 128), jnp.bfloat16),
        pltpu.VMEM((2, 8, depth * 32, 256), jnp.bfloat16),
        pltpu.VMEM((4, 16, 128, 128), jnp.float32),
    ]
    if any(starts[b] for b in blocks):
        operands.append(acc)
        specs.append(anywhere)
    last = pair is not None
    if last:
        operands += [pair, offset]
        specs += [anywhere, whole]
        scratch += [pltpu.VMEM((4, 4, 4, 128, 128), jnp.bfloat16)] * 2
    return pl.pallas_call(
        functools.partial(product_kernel, low, high, starts, last),
        in_specs=[pl.BlockSpec(memory_space=pltpu.SMEM)] + specs,
        out_specs=anywhere,
        scratch_shapes=scratch
        + [
            pltpu.SemaphoreType.DMA((4, 2)),
            pltpu.SemaphoreType.DMA((len(right),)),
            pltpu.SemaphoreType.DMA((4,)),
            pltpu.SemaphoreType.DMA((4, 4)),
            pltpu.SemaphoreType.DMA((4, 4)),
        ],
        out_shape=jax.ShapeDtypeStruct((64, 128, 128), jnp.bfloat16)
        if last
        else jax.ShapeDtypeStruct((4, 16, 128, 128), jnp.float32),
        compiler_params=pltpu.CompilerParams(vmem_limit_bytes=24 * MIB),
        cost_estimate=pl.CostEstimate(flops=cost * 10**6, bytes_accessed=MIB, transcendentals=0),
        name="product",
    )(place, *operands)


def permute(value, to):
    pairs = []
    for row in range(16):
        for col in range(8):
            other = to((row, col))
            pairs.append((row * 8 + col, other[0] * 8 + other[1]))
    return lax.ppermute(value, ("row", "col"), pairs)


def mask_of(step, core):
    return (1, 3)[(step + core) % 2]


def hop(part, step, index):
    row, col = index
    y, x = row // 4, row % 4
    mask = mask_of(step, col % 2)
    along_x = (step < 2) == (part == 0)
    return (y * 4 + (x ^ mask), col) if along_x else ((y ^ mask) * 4 + x, col)


def offsets(part, steps, core):
    out = 0
    for step in steps:
        mask = mask_of(step, core)
        out ^= mask if (step < 2) == (part == 0) else mask * 4
    return out


def per_device(
    alignment_features,
    standardize_gain,
    standardize_offset,
    first_factor_matrix,
    first_factor_offset,
    second_factor_matrix,
    second_factor_offset,
    final_matrix,
    final_offset,
    pairwise_features,
):
    row, col = lax.axis_index("row"), lax.axis_index("col")
    z, core = col // 2, col % 2
    projected = project(
        alignment_features,
        standardize_gain,
        standardize_offset,
        first_factor_matrix,
        first_factor_offset,
        second_factor_matrix,
        second_factor_offset,
    ).reshape(128, 8, 512)
    received = lax.all_to_all(projected, ("row", "col"), split_axis=0, concat_axis=0, tiled=True)

    order = np.array(
        [
            [
                (offsets(part, steps + extra, which), part)
                for steps in [UNITS[unit] for unit in ORDER]
                for part in range(2)
                for extra in [(), (0,)]
            ]
            for which in range(2)
        ]
    )
    order = jnp.where(core == 0, order[0], order[1])
    channel = (row ^ order[:, 0]) * 2 + order[:, 1]
    weights = (final_matrix / 1024).astype(jnp.bfloat16).reshape(32, 32, 128)
    weights = jnp.transpose(jnp.take(weights, channel, axis=1), (2, 1, 0)).reshape(128, 1024)

    place = jnp.stack([z, z ^ 1, z ^ 3, z ^ 2, core]).astype(jnp.int32)
    received, weights, place = lax.optimization_barrier((received, weights, place))
    own, right = split(received.reshape(1024, 512))

    parts = []
    for part in range(2):
        block = right[part : part + 1]
        unit = jnp.concatenate([block, permute(block, functools.partial(hop, part, 0))], axis=0)
        units = [unit]
        for step in range(1, 4):
            units += [permute(unit, functools.partial(hop, part, step)) for unit in units]
        parts.append(units)

    over_z = lambda value, mask: permute(value, lambda i: (i[0], ((i[1] // 2) ^ mask) * 2 + i[1] % 2))
    over_z_by_core = lambda value: permute(value, lambda i: (i[0], ((i[1] // 2) ^ (3, 1)[i[1] % 2]) * 2 + i[1] % 2))
    near, far = over_z(own, 1), over_z(own, 3)
    opposite = over_z_by_core(jnp.where(core == 0, near, far))
    left = []
    for block in (own, near, far, opposite):
        left.append((block, permute(block, lambda i: (i[0], i[1] ^ 1))))

    acc = None
    for low, high, starts, cost in PRODUCTS:
        last = high == 8
        acc = product(
            place,
            left,
            [parts[part][unit] for unit in ORDER[low:high] for part in range(2)],
            low,
            high,
            starts,
            cost,
            weights,
            acc,
            pairwise_features if last else None,
            final_offset.reshape(1, 128) if last else None,
        )
    return acc


def solution(mesh):
    placed = (
        P(("row", "col"), None, None),
        P(),
        P(),
        P(),
        P(),
        P(),
        P(),
        P(),
        P(),
        P("row", "col", None),
    )
    return jax.shard_map(
        per_device, mesh=mesh, in_specs=placed, out_specs=P("row", "col", None), check_vma=False
    )
```

time: 454 us -> 116 us (0.26)
  waiting for transfers between devices: 254 us -> 36.3 us
  local copies, waits for them, and re-layouts: 76.8 us -> 2.98 us
  matrix products: 46.2 us -> 0 us
  blocking collectives: 42.6 us -> 0 us
  Pallas kernels: 0 us -> 41.8 us
  starting transfers between devices: 0.04 us -> 31.2 us
  other arithmetic: 19.1 us -> 2.58 us
  between operations: 13.6 us -> 0.42 us
    all_gather x2 -> x0, waiting for transfers between devices: 254 us -> none  [the longest x1 192 us: per_device(): right_tile = lax.all_gather(right_moved, 'row', axis=1, tiled=True)]
    dot_general x10 -> x0, matrix products: 46.2 us -> none  [the longest x4 32.9 us: one_block(): jnp.einsum('sic,sje->ijce', left_piece, right_tile, preferred_element_typ...]
    all_to_all x2 -> x0, blocking collectives: 42.6 us -> none  [the longest x1 24.7 us: per_device(): lax.all_to_all(left, ('row', 'col'), split_axis=1, concat_axis=0, tiled=T...]
    pallas_call x0 -> x5, Pallas kernels: none -> 41.8 us  [the longest x3 33.9 us: product(): pl.pallas_call(functools.partial(product_kernel, low, high, starts, last)...]
    while x1 -> x0, local copies, waits for them, and re-layouts: 30.8 us -> none  [per_device(): result = lax.map(one_block, (left_blocks, pair_blocks))]
    ppermute x0 -> x23, starting transfers between devices: none -> 20.1 us  [permute(): return lax.ppermute(value, ('row', 'col'), pairs)]
    reshape x2 -> x1, local copies, waits for them, and re-layouts: 19.2 us -> 0.11 us  [per_device(): weights = (final_matrix / 1024).astype(jnp.bfloat16).reshape(32, 32, 128)]
    ppermute x0 -> x23, waiting for transfers between devices: none -> 18.7 us  [permute(): return lax.ppermute(value, ('row', 'col'), pairs)]
  transfers between devices with their start and end apart: 2 -> 24, of which waited for: 2 -> 11; matrix products, arithmetic and copies ran while one was open for 6% -> 4% of each run, Pallas kernels for 0% -> 17%
where the time goes in v2:
time: 116 us; the launch traced here: 115 us
  Pallas kernels  41.8 us (36%)
  waiting for transfers between devices  36.3 us (31%)
  starting transfers between devices  31.2 us (27%)
  local copies, waits for them, and re-layouts  2.98 us (3%)
  other arithmetic  2.58 us (2%)
    pallas_call x3, Pallas kernels, product(): pl.pallas_call(functools.partial(product_kernel, low, high, starts, last)...  33.9 us
    ppermute x23, starting transfers between devices, permute(): return lax.ppermute(value, ('row', 'col'), pairs)  20.1 us
    ppermute x23, waiting for transfers between devices, permute(): return lax.ppermute(value, ('row', 'col'), pairs)  18.7 us
    all_to_all x1, waiting for transfers between devices, per_device(): lax.all_to_all(projected, ('row', 'col'), split_axis=0, concat_axis=0, ti...  17.6 us
    all_to_all x1, starting transfers between devices, per_device(): lax.all_to_all(projected, ('row', 'col'), split_axis=0, concat_axis=0, ti...  11.2 us
    pallas_call x1, Pallas kernels, project(): pl.pallas_call(project_kernel, in_specs=[pl.BlockSpec(memory_space=pl.ANY...  7.72 us
  transfers between devices with their start and end apart: 24, of which 11 were waited for; matrix products, arithmetic and copies ran while one was open for 4% of the time, Pallas kernels for 17%

profile of v2, /device:TPU:0, one launch (start us, length us, event | category | flops | bytes accessed | tf_op | source)
XLA Modules:
  0.0 115.3 jit_solution(4297250771766376444)
XLA Ops:
  0.0 7.7 %project.1 = bf16[16,8,8,512]{3,2,1,0:T(8,128)(2,1)} custom-call(bf16[8,1024,256]{2,1,0:T(8,128)(2,1)} %x_ref.1, f32[1,256]{1,0:T(1,128)} %bitcast.29, f32[1,256]{1,0:T(1,128)} %bitcast.30, bf16[32,256]{1,0:T(8,128)(2,1)} %bitcast.26, f32[1,32]{1,0:T(1,128)} %bitcast.31, bf16[32,256]{1,0:T(8,128)(2,1)} %bitcast.27, f32[1,32]{1,0:T(1,128)} %bitcast.32), custom_call_target="tpu_custom_call" | custom-call | tf_op jit(solution)/shard_map/project/pallas_call | solution.py:63
  7.7 11.2 %all-to-all-start = ((bf16[128,8,512]{2,1,0:T(8,128)(2,1)}), bf16[128,8,512]{2,1,0:T(8,128)(2,1)S(1)}, u32[]{:S(2)}, u32[]{:S(2)}) async-start(bf16[128,8,512]{2,1,0:T(8,128)(2,1)} %bitcast.23), calls=%async_computation | async-start | bytes 2097152 | tf_op jit(solution)/shard_map/all_to_all | solution.py:310
  20.6 17.6 %all-to-all-done = bf16[128,8,512]{2,1,0:T(8,128)(2,1)S(1)} async-done(((bf16[128,8,512]{2,1,0:T(8,128)(2,1)}), bf16[128,8,512]{2,1,0:T(8,128)(2,1)S(1)}, u32[]{:S(2)}, u32[]{:S(2)}) %all-to-all-start) | async-done | bytes 1048608 | tf_op jit(solution)/shard_map/all_to_all | solution.py:310
  41.3 4.4 %collective-permute-done.10 = bf16[1,1024,128]{2,1,0:T(8,128)(2,1)S(1)} collective-permute-done((bf16[1,1024,128]{2,1,0:T(8,128)(2,1)S(1)}, bf16[1,1024,128]{2,1,0:T(8,128)(2,1)S(1)}, u32[]{:S(2)}, u32[]{:S(2)}) %collective-permute-start.10) | collective-permute-done | bytes 262176 | tf_op jit(solution)/shard_map/ppermute | solution.py:264
  48.2 1.9 %collective-permute-start.8 = (bf16[2,1024,128]{2,1,0:T(8,128)(2,1)}, bf16[2,1024,128]{2,1,0:T(8,128)(2,1)}, u32[]{:S(2)}, u32[]{:S(2)}) collective-permute-start(bf16[2,1024,128]{2,1,0:T(8,128)(2,1)} %pad_maximum_fusion.refs_8_), channel_id=1, source_target_pairs={{0,24},{1,9},{2,26},{3,11},{4,28},{5,13},{6,30},{7,15},{8,16},{9,1... | collective-permute-start | bytes 1572872 | tf_op jit(solution)/shard_map/ppermute | solution.py:264
  50.2 1.5 %collective-permute-done.1.refs_2_ = bf16[256,1024]{1,0:T(8,128)(2,1)S(1)} collective-permute-done((bf16[256,1024]{1,0:T(8,128)(2,1)S(1)}, bf16[256,1024]{1,0:T(8,128)(2,1)S(1)}, u32[]{:S(2)}, u32[]{:S(2)}) %collective-permute-start.1) | collective-permute-done | bytes 524320 | tf_op jit(solution)/shard_map/ppermute | solution.py:264
  51.7 1.3 %collective-permute-done.3.refs_4_ = bf16[256,1024]{1,0:T(8,128)(2,1)S(1)} collective-permute-done((bf16[256,1024]{1,0:T(8,128)(2,1)S(1)}, bf16[256,1024]{1,0:T(8,128)(2,1)S(1)}, u32[]{:S(2)}, u32[]{:S(2)}) %collective-permute-start.3) | collective-permute-done | bytes 524320 | tf_op jit(solution)/shard_map/ppermute | solution.py:264
  55.4 3.3 %collective-permute-done.11.refs_11_ = bf16[2,1024,128]{2,1,0:T(8,128)(2,1)S(1)} collective-permute-done((bf16[2,1024,128]{2,1,0:T(8,128)(2,1)}, bf16[2,1024,128]{2,1,0:T(8,128)(2,1)S(1)}, u32[]{:S(2)}, u32[]{:S(2)}) %collective-permute-start.11) | collective-permute-done | bytes 524320 | tf_op jit(solution)/shard_map/ppermute | solution.py:264
  58.8 2.6 %collective-permute-done.8.refs_10_ = bf16[2,1024,128]{2,1,0:T(8,128)(2,1)} collective-permute-done((bf16[2,1024,128]{2,1,0:T(8,128)(2,1)}, bf16[2,1024,128]{2,1,0:T(8,128)(2,1)}, u32[]{:S(2)}, u32[]{:S(2)}) %collective-permute-start.8) | collective-permute-done | bytes 524320 | tf_op jit(solution)/shard_map/ppermute | solution.py:264
  61.4 2.1 %collective-permute-done.5.refs_6_ = bf16[256,1024]{1,0:T(8,128)(2,1)S(1)} collective-permute-done((bf16[256,1024]{1,0:T(8,128)(2,1)S(1)}, bf16[256,1024]{1,0:T(8,128)(2,1)S(1)}, u32[]{:S(2)}, u32[]{:S(2)}) %collective-permute-start.5) | collective-permute-done | bytes 524320 | tf_op jit(solution)/shard_map/ppermute | solution.py:264
  63.5 1.1 copy.19.refs_12_.refs_14_
  64.6 1.2 %collective-permute-start.21 = (bf16[2,1024,128]{2,1,0:T(8,128)(2,1)}, bf16[2,1024,128]{2,1,0:T(8,128)(2,1)S(1)}, u32[]{:S(2)}, u32[]{:S(2)}) collective-permute-start(bf16[2,1024,128]{2,1,0:T(8,128)(2,1)} %pad_maximum_fusion.refs_8_), channel_id=1, source_target_pairs={{0,96},{1,33},{2,98},{3,35},{4,100},{5,37},{6,102},{7,39},{8,104},... | collective-permute-start | bytes 1572872 | tf_op jit(solution)/shard_map/ppermute | solution.py:264
  65.8 2.1 %collective-permute-start.22 = (bf16[2,1024,128]{2,1,0:T(8,128)(2,1)}, bf16[2,1024,128]{2,1,0:T(8,128)(2,1)S(1)}, u32[]{:S(2)}, u32[]{:S(2)}) collective-permute-start(bf16[2,1024,128]{2,1,0:T(8,128)(2,1)} %pad_maximum_fusion.1.refs_9_), channel_id=1, source_target_pairs={{0,24},{1,9},{2,26},{3,11},{4,28},{5,13},{6,30},{7,15},{8,16},{9,1... | collective-permute-start | bytes 1572872 | tf_op jit(solution)/shard_map/ppermute | solution.py:264
  67.9 1.2 %collective-permute-start.12 = (bf16[2,1024,128]{2,1,0:T(8,128)(2,1)}, bf16[2,1024,128]{2,1,0:T(8,128)(2,1)S(1)}, u32[]{:S(2)}, u32[]{:S(2)}) collective-permute-start(bf16[2,1024,128]{2,1,0:T(8,128)(2,1)} %copy-done.2), channel_id=1, source_target_pairs={{0,24},{1,9},{2,26},{3,11},{4,28},{5,13},{6,30},{7,15},{8,16},{9,1... | collective-permute-start | bytes 1572872 | tf_op jit(solution)/shard_map/ppermute | solution.py:264
  70.2 8.5 %product.3.refs_15_ = f32[4,16,128,128]{3,2,1,0:T(8,128)S(1)} custom-call(s32[5]{0:T(128)S(1)} %stack.23.place_ref, bf16[256,1024]{1,0:T(8,128)(2,1)S(1)} %get-tuple-element.12.refs_0_, bf16[256,1024]{1,0:T(8,128)(2,1)S(1)} %collective-permute-done.refs_1_, bf16[256,1024]{1,0:T(8,128)(2,1)S(1)} %collective-permute-done.1.refs_2_, ...), custom_call_target="tpu_custom_call" | custom-call | flops 8000000000 | bytes 1048576 | tf_op jit(solution)/shard_map/product/pallas_call | solution.py:237
  79.3 1.7 %collective-permute-start.9 = (bf16[2,1024,128]{2,1,0:T(8,128)(2,1)}, bf16[2,1024,128]{2,1,0:T(8,128)(2,1)S(1)}, u32[]{:S(2)}, u32[]{:S(2)}) collective-permute-start(bf16[2,1024,128]{2,1,0:T(8,128)(2,1)} %collective-permute-done.8.refs_10_), channel_id=1, source_target_pairs={{0,96},{1,33},{2,98},{3,35},{4,100},{5,37},{6,102},{7,39},{8,104},... | collective-permute-start | bytes 1572872 | tf_op jit(solution)/shard_map/ppermute | solution.py:264
  81.2 1.3 %collective-permute-start.14 = (bf16[2,1024,128]{2,1,0:T(8,128)(2,1)}, bf16[2,1024,128]{2,1,0:T(8,128)(2,1)S(1)}, u32[]{:S(2)}, u32[]{:S(2)}) collective-permute-start(bf16[2,1024,128]{2,1,0:T(8,128)(2,1)} %collective-permute-done.13.refs_8_), channel_id=1, source_target_pairs={{0,96},{1,33},{2,98},{3,35},{4,100},{5,37},{6,102},{7,39},{8,104},... | collective-permute-start | bytes 1572872 | tf_op jit(solution)/shard_map/ppermute | solution.py:264
  82.5 1.7 %collective-permute-start.16 = (bf16[2,1024,128]{2,1,0:T(8,128)(2,1)}, bf16[2,1024,128]{2,1,0:T(8,128)(2,1)S(1)}, u32[]{:S(2)}, u32[]{:S(2)}) collective-permute-start(bf16[2,1024,128]{2,1,0:T(8,128)(2,1)} %collective-permute-done.15.refs_9_), channel_id=1, source_target_pairs={{0,24},{1,9},{2,26},{3,11},{4,28},{5,13},{6,30},{7,15},{8,16},{9,1... | collective-permute-start | bytes 1572872 | tf_op jit(solution)/shard_map/ppermute | solution.py:264
  84.2 1.6 %collective-permute-start.18 = (bf16[2,1024,128]{2,1,0:T(8,128)(2,1)S(1)}, bf16[2,1024,128]{2,1,0:T(8,128)(2,1)S(1)}, u32[]{:S(2)}, u32[]{:S(2)}) collective-permute-start(bf16[2,1024,128]{2,1,0:T(8,128)(2,1)S(1)} %collective-permute-done.17.refs_12_), channel_id=1, source_target_pairs={{0,96},{1,33},{2,98},{3,35},{4,100},{5,37},{6,102},{7,39},{8,104},... | collective-permute-start | bytes 1572872 | tf_op jit(solution)/shard_map/ppermute | solution.py:264
  85.7 1.1 collective-permute-done.12.refs_9_
  86.8 1.3 %collective-permute-start.20 = (bf16[2,1024,128]{2,1,0:T(8,128)(2,1)S(1)}, bf16[2,1024,128]{2,1,0:T(8,128)(2,1)S(1)}, u32[]{:S(2)}, u32[]{:S(2)}) collective-permute-start(bf16[2,1024,128]{2,1,0:T(8,128)(2,1)S(1)} %collective-permute-done.19.refs_13_), channel_id=1, source_target_pairs={{0,24},{1,9},{2,26},{3,11},{4,28},{5,13},{6,30},{7,15},{8,16},{9,1... | collective-permute-start | bytes 1572872 | tf_op jit(solution)/shard_map/ppermute | solution.py:264
  88.1 11.4 %product.4.refs_15_ = f32[4,16,128,128]{3,2,1,0:T(8,128)S(1)} custom-call(s32[5]{0:T(128)S(1)} %stack.23.place_ref, bf16[256,1024]{1,0:T(8,128)(2,1)S(1)} %get-tuple-element.12.refs_0_, bf16[256,1024]{1,0:T(8,128)(2,1)S(1)} %collective-permute-done.refs_1_, bf16[256,1024]{1,0:T(8,128)(2,1)S(1)} %collective-permute-done.1.refs_2_, ...), custom_call_target="tpu_custom_call" | custom-call | flops 12000000000 | bytes 1048576 | tf_op jit(solution)/shard_map/product/pallas_call | solution.py:237
  99.5 1.6 %collective-permute-done.18.refs_12_ = bf16[2,1024,128]{2,1,0:T(8,128)(2,1)S(1)} collective-permute-done((bf16[2,1024,128]{2,1,0:T(8,128)(2,1)S(1)}, bf16[2,1024,128]{2,1,0:T(8,128)(2,1)S(1)}, u32[]{:S(2)}, u32[]{:S(2)}) %collective-permute-start.18) | collective-permute-done | bytes 524320 | tf_op jit(solution)/shard_map/ppermute | solution.py:264
  101.1 14.0 %product.5 = bf16[64,128,128]{2,1,0:T(8,128)(2,1)} custom-call(s32[5]{0:T(128)S(1)} %stack.23.place_ref, bf16[256,1024]{1,0:T(8,128)(2,1)S(1)} %get-tuple-element.12.refs_0_, bf16[256,1024]{1,0:T(8,128)(2,1)S(1)} %collective-permute-done.refs_1_, bf16[256,1024]{1,0:T(8,128)(2,1)S(1)} %collective-permute-done.1.refs_2_, ...), custom_call_target="tpu_custom_call" | custom-call | flops 80000000 | bytes 1048576 | tf_op jit(solution)/shard_map/product/pallas_call | solution.py:237
  (56 shorter events, 11.7 us)
Async XLA Ops:
  7.7 30.4 %all-to-all-start = ((bf16[128,8,512]{2,1,0:T(8,128)(2,1)}), bf16[128,8,512]{2,1,0:T(8,128)(2,1)S(1)}, u32[]{:S(2)}, u32[]{:S(2)}) async-start(bf16[128,8,512]{2,1,0:T(8,128)(2,1)} %bitcast.23), calls=%async_computation | async-start | bytes 2097152 | tf_op jit(solution)/shard_map/all_to_all | solution.py:310
  38.4 13.2 %collective-permute-start.1 = (bf16[256,1024]{1,0:T(8,128)(2,1)S(1)}, bf16[256,1024]{1,0:T(8,128)(2,1)S(1)}, u32[]{:S(2)}, u32[]{:S(2)}) collective-permute-start(bf16[256,1024]{1,0:T(8,128)(2,1)S(1)} %get-tuple-element.12.refs_0_), channel_id=1, source_target_pairs={{0,2},{1,3},{2,0},{3,1},{4,6},{5,7},{6,4},{7,5},{8,10},{9,11},{10,... | collective-permute-start | bytes 1572872 | tf_op jit(solution)/shard_map/ppermute | solution.py:264
  38.8 14.2 %collective-permute-start.3 = (bf16[256,1024]{1,0:T(8,128)(2,1)S(1)}, bf16[256,1024]{1,0:T(8,128)(2,1)S(1)}, u32[]{:S(2)}, u32[]{:S(2)}) collective-permute-start(bf16[256,1024]{1,0:T(8,128)(2,1)S(1)} %get-tuple-element.12.refs_0_), channel_id=1, source_target_pairs={{0,6},{1,7},{2,4},{3,5},{4,2},{5,3},{6,0},{7,1},{8,14},{9,15},{10,... | collective-permute-start | bytes 1572872 | tf_op jit(solution)/shard_map/ppermute | solution.py:264
  39.3 6.5 %collective-permute-start.10 = (bf16[1,1024,128]{2,1,0:T(8,128)(2,1)S(1)}, bf16[1,1024,128]{2,1,0:T(8,128)(2,1)S(1)}, u32[]{:S(2)}, u32[]{:S(2)}) collective-permute-start(bf16[1,1024,128]{2,1,0:T(8,128)(2,1)S(1)} %get-tuple-element.17), channel_id=1, source_target_pairs={{0,32},{1,97},{2,34},{3,99},{4,36},{5,101},{6,38},{7,103},{8,40},{... | collective-permute-start | bytes 786440 | tf_op jit(solution)/shard_map/ppermute | solution.py:264
  39.7 7.7 %collective-permute-start.7 = (bf16[1,1024,128]{2,1,0:T(8,128)(2,1)S(1)}, bf16[1,1024,128]{2,1,0:T(8,128)(2,1)S(1)}, u32[]{:S(2)}, u32[]{:S(2)}) collective-permute-start(bf16[1,1024,128]{2,1,0:T(8,128)(2,1)S(1)} %get-tuple-element.18), channel_id=1, source_target_pairs={{0,8},{1,25},{2,10},{3,27},{4,12},{5,29},{6,14},{7,31},{8,0},{9,17... | collective-permute-start | bytes 786440 | tf_op jit(solution)/shard_map/ppermute | solution.py:264
  40.4 14.2 %collective-permute-start = (bf16[256,1024]{1,0:T(8,128)(2,1)S(1)}, bf16[256,1024]{1,0:T(8,128)(2,1)S(1)}, u32[]{:S(2)}, u32[]{:S(2)}) collective-permute-start(bf16[256,1024]{1,0:T(8,128)(2,1)S(1)} %get-tuple-element.12.refs_0_), channel_id=1, source_target_pairs={{0,1},{1,0},{2,3},{3,2},{4,5},{5,4},{6,7},{7,6},{8,9},{9,8},{10,11... | collective-permute-start | bytes 1572872 | tf_op jit(solution)/shard_map/ppermute | solution.py:264
  46.5 12.2 %collective-permute-start.11 = (bf16[2,1024,128]{2,1,0:T(8,128)(2,1)}, bf16[2,1024,128]{2,1,0:T(8,128)(2,1)S(1)}, u32[]{:S(2)}, u32[]{:S(2)}) collective-permute-start(bf16[2,1024,128]{2,1,0:T(8,128)(2,1)} %pad_maximum_fusion.1.refs_9_), channel_id=1, source_target_pairs={{0,96},{1,33},{2,98},{3,35},{4,100},{5,37},{6,102},{7,39},{8,104},... | collective-permute-start | bytes 1572872 | tf_op jit(solution)/shard_map/ppermute | solution.py:264
  48.2 13.2 %collective-permute-start.8 = (bf16[2,1024,128]{2,1,0:T(8,128)(2,1)}, bf16[2,1024,128]{2,1,0:T(8,128)(2,1)}, u32[]{:S(2)}, u32[]{:S(2)}) collective-permute-start(bf16[2,1024,128]{2,1,0:T(8,128)(2,1)} %pad_maximum_fusion.refs_8_), channel_id=1, source_target_pairs={{0,24},{1,9},{2,26},{3,11},{4,28},{5,13},{6,30},{7,15},{8,16},{9,1... | collective-permute-start | bytes 1572872 | tf_op jit(solution)/shard_map/ppermute | solution.py:264
  53.0 10.5 %collective-permute-start.5 = (bf16[256,1024]{1,0:T(8,128)(2,1)S(1)}, bf16[256,1024]{1,0:T(8,128)(2,1)S(1)}, u32[]{:S(2)}, u32[]{:S(2)}) collective-permute-start(bf16[256,1024]{1,0:T(8,128)(2,1)S(1)} %broadcast_select_fusion), channel_id=1, source_target_pairs={{0,6},{1,3},{2,4},{3,1},{4,2},{5,7},{6,0},{7,5},{8,14},{9,11},{10,... | collective-permute-start | bytes 1572872 | tf_op jit(solution)/shard_map/ppermute | solution.py:264
  54.0 10.6 %collective-permute-start.13 = (bf16[2,1024,128]{2,1,0:T(8,128)(2,1)}, bf16[2,1024,128]{2,1,0:T(8,128)(2,1)}, u32[]{:S(2)}, u32[]{:S(2)}) collective-permute-start(bf16[2,1024,128]{2,1,0:T(8,128)(2,1)} %pad_maximum_fusion.refs_8_), channel_id=1, source_target_pairs={{0,32},{1,97},{2,34},{3,99},{4,36},{5,101},{6,38},{7,103},{8,40},{... | collective-permute-start | bytes 1572872 | tf_op jit(solution)/shard_map/ppermute | solution.py:264
  54.6 11.2 %collective-permute-start.15 = (bf16[2,1024,128]{2,1,0:T(8,128)(2,1)}, bf16[2,1024,128]{2,1,0:T(8,128)(2,1)}, u32[]{:S(2)}, u32[]{:S(2)}) collective-permute-start(bf16[2,1024,128]{2,1,0:T(8,128)(2,1)} %pad_maximum_fusion.1.refs_9_), channel_id=1, source_target_pairs={{0,8},{1,25},{2,10},{3,27},{4,12},{5,29},{6,14},{7,31},{8,0},{9,17... | collective-permute-start | bytes 1572872 | tf_op jit(solution)/shard_map/ppermute | solution.py:264
  58.8 9.2 %collective-permute-start.2 = (bf16[256,1024]{1,0:T(8,128)(2,1)S(1)}, bf16[256,1024]{1,0:T(8,128)(2,1)S(1)}, u32[]{:S(2)}, u32[]{:S(2)}) collective-permute-start(bf16[256,1024]{1,0:T(8,128)(2,1)S(1)} %collective-permute-done.1.refs_2_), channel_id=1, source_target_pairs={{0,1},{1,0},{2,3},{3,2},{4,5},{5,4},{6,7},{7,6},{8,9},{9,8},{10,11... | collective-permute-start | bytes 1572872 | tf_op jit(solution)/shard_map/ppermute | solution.py:264
  61.4 6.5 %collective-permute-start.4 = (bf16[256,1024]{1,0:T(8,128)(2,1)S(1)}, bf16[256,1024]{1,0:T(8,128)(2,1)}, u32[]{:S(2)}, u32[]{:S(2)}) collective-permute-start(bf16[256,1024]{1,0:T(8,128)(2,1)S(1)} %collective-permute-done.3.refs_4_), channel_id=1, source_target_pairs={{0,1},{1,0},{2,3},{3,2},{4,5},{5,4},{6,7},{7,6},{8,9},{9,8},{10,11... | collective-permute-start | bytes 1572872 | tf_op jit(solution)/shard_map/ppermute | solution.py:264
  63.5 5.6 %collective-permute-start.6 = (bf16[256,1024]{1,0:T(8,128)(2,1)S(1)}, bf16[256,1024]{1,0:T(8,128)(2,1)}, u32[]{:S(2)}, u32[]{:S(2)}) collective-permute-start(bf16[256,1024]{1,0:T(8,128)(2,1)S(1)} %collective-permute-done.5.refs_6_), channel_id=1, source_target_pairs={{0,1},{1,0},{2,3},{3,2},{4,5},{5,4},{6,7},{7,6},{8,9},{9,8},{10,11... | collective-permute-start | bytes 1572872 | tf_op jit(solution)/shard_map/ppermute | solution.py:264
  64.6 14.7 %collective-permute-start.21 = (bf16[2,1024,128]{2,1,0:T(8,128)(2,1)}, bf16[2,1024,128]{2,1,0:T(8,128)(2,1)S(1)}, u32[]{:S(2)}, u32[]{:S(2)}) collective-permute-start(bf16[2,1024,128]{2,1,0:T(8,128)(2,1)} %pad_maximum_fusion.refs_8_), channel_id=1, source_target_pairs={{0,96},{1,33},{2,98},{3,35},{4,100},{5,37},{6,102},{7,39},{8,104},... | collective-permute-start | bytes 1572872 | tf_op jit(solution)/shard_map/ppermute | solution.py:264
  65.8 15.4 %collective-permute-start.22 = (bf16[2,1024,128]{2,1,0:T(8,128)(2,1)}, bf16[2,1024,128]{2,1,0:T(8,128)(2,1)S(1)}, u32[]{:S(2)}, u32[]{:S(2)}) collective-permute-start(bf16[2,1024,128]{2,1,0:T(8,128)(2,1)} %pad_maximum_fusion.1.refs_9_), channel_id=1, source_target_pairs={{0,24},{1,9},{2,26},{3,11},{4,28},{5,13},{6,30},{7,15},{8,16},{9,1... | collective-permute-start | bytes 1572872 | tf_op jit(solution)/shard_map/ppermute | solution.py:264
  67.9 16.2 %collective-permute-start.19 = (bf16[2,1024,128]{2,1,0:T(8,128)(2,1)}, bf16[2,1024,128]{2,1,0:T(8,128)(2,1)S(1)}, u32[]{:S(2)}, u32[]{:S(2)}) collective-permute-start(bf16[2,1024,128]{2,1,0:T(8,128)(2,1)} %copy-done.2), channel_id=1, source_target_pairs={{0,8},{1,25},{2,10},{3,27},{4,12},{5,29},{6,14},{7,31},{8,0},{9,17... | collective-permute-start | bytes 1572872 | tf_op jit(solution)/shard_map/ppermute | solution.py:264
  67.9 18.9 %collective-permute-start.12 = (bf16[2,1024,128]{2,1,0:T(8,128)(2,1)}, bf16[2,1024,128]{2,1,0:T(8,128)(2,1)S(1)}, u32[]{:S(2)}, u32[]{:S(2)}) collective-permute-start(bf16[2,1024,128]{2,1,0:T(8,128)(2,1)} %copy-done.2), channel_id=1, source_target_pairs={{0,24},{1,9},{2,26},{3,11},{4,28},{5,13},{6,30},{7,15},{8,16},{9,1... | collective-permute-start | bytes 1572872 | tf_op jit(solution)/shard_map/ppermute | solution.py:264
  69.1 13.4 %collective-permute-start.17 = (bf16[2,1024,128]{2,1,0:T(8,128)(2,1)}, bf16[2,1024,128]{2,1,0:T(8,128)(2,1)S(1)}, u32[]{:S(2)}, u32[]{:S(2)}) collective-permute-start(bf16[2,1024,128]{2,1,0:T(8,128)(2,1)} %collective-permute-done.8.refs_10_), channel_id=1, source_target_pairs={{0,32},{1,97},{2,34},{3,99},{4,36},{5,101},{6,38},{7,103},{8,40},{... | collective-permute-start | bytes 1572872 | tf_op jit(solution)/shard_map/ppermute | solution.py:264
  79.3 20.3 %collective-permute-start.9 = (bf16[2,1024,128]{2,1,0:T(8,128)(2,1)}, bf16[2,1024,128]{2,1,0:T(8,128)(2,1)S(1)}, u32[]{:S(2)}, u32[]{:S(2)}) collective-permute-start(bf16[2,1024,128]{2,1,0:T(8,128)(2,1)} %collective-permute-done.8.refs_10_), channel_id=1, source_target_pairs={{0,96},{1,33},{2,98},{3,35},{4,100},{5,37},{6,102},{7,39},{8,104},... | collective-permute-start | bytes 1572872 | tf_op jit(solution)/shard_map/ppermute | solution.py:264
  81.2 18.3 %collective-permute-start.14 = (bf16[2,1024,128]{2,1,0:T(8,128)(2,1)}, bf16[2,1024,128]{2,1,0:T(8,128)(2,1)S(1)}, u32[]{:S(2)}, u32[]{:S(2)}) collective-permute-start(bf16[2,1024,128]{2,1,0:T(8,128)(2,1)} %collective-permute-done.13.refs_8_), channel_id=1, source_target_pairs={{0,96},{1,33},{2,98},{3,35},{4,100},{5,37},{6,102},{7,39},{8,104},... | collective-permute-start | bytes 1572872 | tf_op jit(solution)/shard_map/ppermute | solution.py:264
  82.5 17.0 %collective-permute-start.16 = (bf16[2,1024,128]{2,1,0:T(8,128)(2,1)}, bf16[2,1024,128]{2,1,0:T(8,128)(2,1)S(1)}, u32[]{:S(2)}, u32[]{:S(2)}) collective-permute-start(bf16[2,1024,128]{2,1,0:T(8,128)(2,1)} %collective-permute-done.15.refs_9_), channel_id=1, source_target_pairs={{0,24},{1,9},{2,26},{3,11},{4,28},{5,13},{6,30},{7,15},{8,16},{9,1... | collective-permute-start | bytes 1572872 | tf_op jit(solution)/shard_map/ppermute | solution.py:264
  84.2 16.9 %collective-permute-start.18 = (bf16[2,1024,128]{2,1,0:T(8,128)(2,1)S(1)}, bf16[2,1024,128]{2,1,0:T(8,128)(2,1)S(1)}, u32[]{:S(2)}, u32[]{:S(2)}) collective-permute-start(bf16[2,1024,128]{2,1,0:T(8,128)(2,1)S(1)} %collective-permute-done.17.refs_12_), channel_id=1, source_target_pairs={{0,96},{1,33},{2,98},{3,35},{4,100},{5,37},{6,102},{7,39},{8,104},... | collective-permute-start | bytes 1572872 | tf_op jit(solution)/shard_map/ppermute | solution.py:264
  86.8 14.3 %collective-permute-start.20 = (bf16[2,1024,128]{2,1,0:T(8,128)(2,1)S(1)}, bf16[2,1024,128]{2,1,0:T(8,128)(2,1)S(1)}, u32[]{:S(2)}, u32[]{:S(2)}) collective-permute-start(bf16[2,1024,128]{2,1,0:T(8,128)(2,1)S(1)} %collective-permute-done.19.refs_13_), channel_id=1, source_target_pairs={{0,24},{1,9},{2,26},{3,11},{4,28},{5,13},{6,30},{7,15},{8,16},{9,1... | collective-permute-start | bytes 1572872 | tf_op jit(solution)/shard_map/ppermute | solution.py:264
  (7 other events, 107.6 us)

commit v3 on v2

--- a/solution.py
+++ b/solution.py
@@ -12,8 +12,9 @@
 UNITS = [()]
 for _step in range(1, 4):
     UNITS += [steps + (_step,) for steps in UNITS]
-ORDER = (0,1,2,4,3,5,6,7)
-PRODUCTS = ((0,2,(0,0,0,0),8000),(2,5,(2,2,2,2),12000),(5,8,(5,5,5,5),80))
+ORDER = (0,1,2,3,4,5,6,7)
+TIED = 0
+PRODUCTS = ((0,2,(0,0,0,None),8000),(0,6,(2,2,2,0),8000),(6,8,(6,6,6,6),80))
 
 
 def project_kernel(x_ref, gain_ref, offset_ref, first_ref, first_offset_ref, second_ref, second_offset_ref, out_ref, held, left, right, ready):
@@ -104,11 +105,11 @@
     )(received)
 
 
-def product_kernel(low, high, starts, last, place_ref, *refs):
+def product_kernel(low, high, right_at, starts, last, place_ref, *refs):
     refs = list(refs)
     blocks = [b for b in range(4) if starts[b] is not None]
     left_refs = {b: (refs.pop(0), refs.pop(0)) for b in blocks}
-    right_refs = [refs.pop(0) for _ in range(2 * (high - low))]
+    right_refs = [refs.pop(0) for _ in range(max(index for index, _ in right_at) + 1)]
     weights_ref = refs.pop(0)
     adds = any(starts[b] for b in blocks)
     acc_ref = refs.pop(0) if adds else None
@@ -124,7 +125,9 @@
         return pltpu.make_async_copy(left_refs[b][theirs], left.at[pl.ds(rows, 256)], left_sem.at[b, theirs])
 
     def right_copy(n):
-        return pltpu.make_async_copy(right_refs[n], right.at[pl.ds(2 * n, 2)], right_sem.at[n])
+        index, offset = right_at[n]
+        source = right_refs[index].at[pl.ds(offset, 2)]
+        return pltpu.make_async_copy(source, right.at[pl.ds(2 * n, 2)], right_sem.at[n])
 
     def acc_copy(b):
         return pltpu.make_async_copy(acc_ref.at[b], total.at[b], acc_sem.at[b])
@@ -144,7 +147,7 @@
         for theirs in range(2):
             left_copy(b, theirs).start()
         if b == blocks[0]:
-            for n in range(len(right_refs)):
+            for n in range(2 * (high - low)):
                 right_copy(n).start()
         if starts[b]:
             acc_copy(b).start()
@@ -177,10 +180,11 @@
             for theirs in range(2):
                 left_copy(b, theirs).wait()
         if n == 1:
-            for other in blocks:
-                if other != blocks[0]:
-                    for theirs in range(2):
-                        left_copy(other, theirs).wait()
+            for other in blocks[1:]:
+                for theirs in range(2):
+                    left_copy(other, theirs).wait()
+        if n in (1, 2):
+            for other in blocks[:1] if n == 1 else blocks[1:]:
                 if starts[other]:
                     acc_copy(other).wait()
                 if last:
@@ -217,7 +221,12 @@
     blocks = [b for b in range(4) if starts[b] is not None]
     anywhere = pl.BlockSpec(memory_space=pl.ANY)
     whole = pl.BlockSpec(memory_space=pltpu.VMEM)
-    operands = [piece for b in blocks for piece in left[b]] + right
+    arrays, right_at = [], []
+    for array, at in right:
+        if not any(array is other for other in arrays):
+            arrays.append(array)
+        right_at.append(([array is other for other in arrays].index(True), at))
+    operands = [piece for b in blocks for piece in left[b]] + arrays
     specs = [anywhere] * len(operands) + [whole]
     operands.append(weights)
     scratch = [
@@ -235,7 +244,7 @@
         specs += [anywhere, whole]
         scratch += [pltpu.VMEM((4, 4, 4, 128, 128), jnp.bfloat16)] * 2
     return pl.pallas_call(
-        functools.partial(product_kernel, low, high, starts, last),
+        functools.partial(product_kernel, low, high, right_at, starts, last),
         in_specs=[pl.BlockSpec(memory_space=pltpu.SMEM)] + specs,
         out_specs=anywhere,
         scratch_shapes=scratch
@@ -249,7 +258,7 @@
         out_shape=jax.ShapeDtypeStruct((64, 128, 128), jnp.bfloat16)
         if last
         else jax.ShapeDtypeStruct((4, 16, 128, 128), jnp.float32),
-        compiler_params=pltpu.CompilerParams(vmem_limit_bytes=24 * MIB),
+        compiler_params=pltpu.CompilerParams(vmem_limit_bytes=(20 if last else 26) * MIB),
         cost_estimate=pl.CostEstimate(flops=cost * 10**6, bytes_accessed=MIB, transcendentals=0),
         name="product",
     )(place, *operands)
@@ -329,14 +338,17 @@
     received, weights, place = lax.optimization_barrier((received, weights, place))
     own, right = split(received.reshape(1024, 512))
 
-    parts = []
-    for part in range(2):
-        block = right[part : part + 1]
-        unit = jnp.concatenate([block, permute(block, functools.partial(hop, part, 0))], axis=0)
-        units = [unit]
-        for step in range(1, 4):
-            units += [permute(unit, functools.partial(hop, part, step)) for unit in units]
-        parts.append(units)
+    def send(blocks, step):
+        return [permute(blocks[part], functools.partial(hop, part, step)) for part in range(2)]
+
+    def join(first, second):
+        return [jnp.concatenate(both, axis=0) for both in zip(first, second)]
+
+    block = [right[part : part + 1] for part in range(2)]
+    two = join(block, send(block, 0))
+    two_more = send(two, 1)
+    third = [send(two, 2), send(two_more, 2)]
+    fourth = send(join(two, two_more), 3)
 
     over_z = lambda value, mask: permute(value, lambda i: (i[0], ((i[1] // 2) ^ mask) * 2 + i[1] % 2))
     over_z_by_core = lambda value: permute(value, lambda i: (i[0], ((i[1] // 2) ^ (3, 1)[i[1] % 2]) * 2 + i[1] % 2))
@@ -347,12 +359,13 @@
         left.append((block, permute(block, lambda i: (i[0], i[1] ^ 1))))
 
     acc = None
-    for low, high, starts, cost in PRODUCTS:
+    units = [(two, 0), (two_more, 0), (third[0], 0), (third[1], 0), (fourth, 0), (fourth, 2)]
+    for number, (low, high, starts, cost) in enumerate(PRODUCTS):
         last = high == 8
         acc = product(
             place,
             left,
-            [parts[part][unit] for unit in ORDER[low:high] for part in range(2)],
+            [(blocks[part], at) for blocks, at in units[low:high] for part in range(2)],
             low,
             high,
             starts,
@@ -362,6 +375,10 @@
             pairwise_features if last else None,
             final_offset.reshape(1, 128) if last else None,
         )
+        if number == TIED:
+            acc, third = lax.optimization_barrier((acc, third))
+            fifth = send(join(*third), 3)
+            units = units[:2] + [(third[0], 0), (third[1], 0)] + units[4:] + [(fifth, 0), (fifth, 2)]
     return acc
 
 

time: 116 us -> 114 us (0.983)
  starting transfers between devices: 31.2 us -> 24.9 us
  waiting for transfers between devices: 36.3 us -> 39.9 us
    ppermute x23 -> x19, starting transfers between devices: 20.1 us -> 13.7 us  [permute(): return lax.ppermute(value, ('row', 'col'), pairs)]
    ppermute x23 -> x19, waiting for transfers between devices: 18.7 us -> 22.4 us  [permute(): return lax.ppermute(value, ('row', 'col'), pairs)]
    concatenate x2 -> x6, other arithmetic: 1.67 us -> 2.55 us  [join(): return [jnp.concatenate(both, axis=0) for both in zip(first, second)]]
  transfers between devices with their start and end apart: 24 -> 20, of which waited for: 11 -> 9; matrix products, arithmetic and copies ran while one was open for 4% -> 5% of each run, Pallas kernels for 17% -> 19%
where the time goes in v3:
time: 114 us; the launch traced here: 113 us
  Pallas kernels  42 us (37%)
  waiting for transfers between devices  39.9 us (35%)
  starting transfers between devices  24.9 us (22%)
  other arithmetic  3.47 us (3%)
  local copies, waits for them, and re-layouts  2.67 us (2%)
    pallas_call x3, Pallas kernels, product(): pl.pallas_call(functools.partial(product_kernel, low, high, right_at, sta...  33.3 us
    ppermute x19, waiting for transfers between devices, permute(): return lax.ppermute(value, ('row', 'col'), pairs)  22.4 us
    all_to_all x1, waiting for transfers between devices, per_device(): lax.all_to_all(projected, ('row', 'col'), split_axis=0, concat_axis=0, ti...  17.5 us
    ppermute x19, starting transfers between devices, permute(): return lax.ppermute(value, ('row', 'col'), pairs)  13.7 us
    all_to_all x1, starting transfers between devices, per_device(): lax.all_to_all(projected, ('row', 'col'), split_axis=0, concat_axis=0, ti...  11.2 us
    pallas_call x1, Pallas kernels, project(): pl.pallas_call(project_kernel, in_specs=[pl.BlockSpec(memory_space=pl.ANY...  7.72 us
    concatenate x6, other arithmetic, join(): return [jnp.concatenate(both, axis=0) for both in zip(first, second)]  2.55 us
  transfers between devices with their start and end apart: 20, of which 9 were waited for; matrix products, arithmetic and copies ran while one was open for 5% of the time, Pallas kernels for 19%

profile of v3, /device:TPU:0, one launch (start us, length us, event | category | flops | bytes accessed | tf_op | source)
XLA Modules:
  0.0 113.4 jit_solution(3987952764662232178)
XLA Ops:
  0.0 7.7 %project.1 = bf16[16,8,8,512]{3,2,1,0:T(8,128)(2,1)} custom-call(bf16[8,1024,256]{2,1,0:T(8,128)(2,1)} %x_ref.1, f32[1,256]{1,0:T(1,128)} %bitcast.29, f32[1,256]{1,0:T(1,128)} %bitcast.30, bf16[32,256]{1,0:T(8,128)(2,1)} %bitcast.26, f32[1,32]{1,0:T(1,128)} %bitcast.31, bf16[32,256]{1,0:T(8,128)(2,1)} %bitcast.27, f32[1,32]{1,0:T(1,128)} %bitcast.32), custom_call_target="tpu_custom_call" | custom-call | tf_op jit(solution)/shard_map/project/pallas_call | solution.py:64
  7.7 11.2 %all-to-all-start = ((bf16[128,8,512]{2,1,0:T(8,128)(2,1)}), bf16[128,8,512]{2,1,0:T(8,128)(2,1)S(1)}, u32[]{:S(2)}, u32[]{:S(2)}) async-start(bf16[128,8,512]{2,1,0:T(8,128)(2,1)} %bitcast.23), calls=%async_computation | async-start | bytes 2097152 | tf_op jit(solution)/shard_map/all_to_all | solution.py:319
  19.8 0.8 broadcast_select_fusion.1
  20.6 17.5 %all-to-all-done = bf16[128,8,512]{2,1,0:T(8,128)(2,1)S(1)} async-done(((bf16[128,8,512]{2,1,0:T(8,128)(2,1)}), bf16[128,8,512]{2,1,0:T(8,128)(2,1)S(1)}, u32[]{:S(2)}, u32[]{:S(2)}) %all-to-all-start) | async-done | bytes 1048608 | tf_op jit(solution)/shard_map/all_to_all | solution.py:319
  38.2 1.1 split.1
  40.7 5.1 %collective-permute-done.8 = bf16[1,1024,128]{2,1,0:T(8,128)(2,1)S(1)} collective-permute-done((bf16[1,1024,128]{2,1,0:T(8,128)(2,1)S(1)}, bf16[1,1024,128]{2,1,0:T(8,128)(2,1)S(1)}, u32[]{:S(2)}, u32[]{:S(2)}) %collective-permute-start.8) | collective-permute-done | bytes 262176 | tf_op jit(solution)/shard_map/ppermute | solution.py:273
  46.5 1.2 %collective-permute-start.10 = (bf16[2,1024,128]{2,1,0:T(8,128)(2,1)S(1)}, bf16[2,1024,128]{2,1,0:T(8,128)(2,1)S(1)}, u32[]{:S(2)}, u32[]{:S(2)}) collective-permute-start(bf16[2,1024,128]{2,1,0:T(8,128)(2,1)S(1)} %pad_maximum_fusion.5.refs_7_.refs_9_), channel_id=1, source_target_pairs={{0,96},{1,33},{2,98},{3,35},{4,100},{5,37},{6,102},{7,39},{8,104},... | collective-permute-start | bytes 1572872 | tf_op jit(solution)/shard_map/ppermute | solution.py:273
  48.6 1.1 copy.17.refs_10_.refs_18_
  49.6 5.7 %collective-permute-done.3.refs_4_ = bf16[256,1024]{1,0:T(8,128)(2,1)S(1)} collective-permute-done((bf16[256,1024]{1,0:T(8,128)(2,1)}, bf16[256,1024]{1,0:T(8,128)(2,1)S(1)}, u32[]{:S(2)}, u32[]{:S(2)}) %collective-permute-start.3) | collective-permute-done | bytes 524320 | tf_op jit(solution)/shard_map/ppermute | solution.py:273
  55.7 1.3 %collective-permute-done.10.refs_9_.refs_11_ = bf16[2,1024,128]{2,1,0:T(8,128)(2,1)S(1)} collective-permute-done((bf16[2,1024,128]{2,1,0:T(8,128)(2,1)S(1)}, bf16[2,1024,128]{2,1,0:T(8,128)(2,1)S(1)}, u32[]{:S(2)}, u32[]{:S(2)}) %collective-permute-start.10) | collective-permute-done | bytes 524320 | tf_op jit(solution)/shard_map/ppermute | solution.py:273
  57.0 1.1 collective-permute-start.4
  58.7 1.1 %pad_maximum_fusion.3 = bf16[4,1024,128]{2,1,0:T(8,128)(2,1)S(1)} fusion(bf16[2,1024,128]{2,1,0:T(8,128)(2,1)S(1)} %collective-permute-done.10.refs_9_.refs_11_, bf16[1,1024,128]{2,1,0:T(8,128)(2,1)} %copy-done.4, bf16[1,1024,128]{2,1,0:T(8,128)(2,1)} %copy-done.3), kind=kLoop, calls=%fused_computation.4 | loop fusion | flops 1048576 | bytes 2097152 | tf_op jit(solution)/shard_map/concatenate | solution.py:345
  59.8 1.1 %pad_maximum_fusion.2 = bf16[4,1024,128]{2,1,0:T(8,128)(2,1)S(1)} fusion(bf16[2,1024,128]{2,1,0:T(8,128)(2,1)S(1)} %collective-permute-done.9.refs_8_.refs_10_, bf16[1,1024,128]{2,1,0:T(8,128)(2,1)} %copy-done.5, bf16[1,1024,128]{2,1,0:T(8,128)(2,1)} %copy-done.2), kind=kLoop, calls=%fused_computation.3 | loop fusion | flops 1048576 | bytes 2097152 | tf_op jit(solution)/shard_map/concatenate | solution.py:345
  61.0 0.8 collective-permute-start.5
  61.8 2.8 %collective-permute-done.12.refs_13_ = bf16[2,1024,128]{2,1,0:T(8,128)(2,1)S(1)} collective-permute-done((bf16[2,1024,128]{2,1,0:T(8,128)(2,1)S(1)}, bf16[2,1024,128]{2,1,0:T(8,128)(2,1)S(1)}, u32[]{:S(2)}, u32[]{:S(2)}) %collective-permute-start.12) | collective-permute-done | bytes 524320 | tf_op jit(solution)/shard_map/ppermute | solution.py:273
  64.6 1.9 %collective-permute-start.17 = (bf16[4,1024,128]{2,1,0:T(8,128)(2,1)S(1)}, bf16[4,1024,128]{2,1,0:T(8,128)(2,1)S(1)}, u32[]{:S(2)}, u32[]{:S(2)}) collective-permute-start(bf16[4,1024,128]{2,1,0:T(8,128)(2,1)S(1)} %pad_maximum_fusion.2), channel_id=1, source_target_pairs={{0,96},{1,33},{2,98},{3,35},{4,100},{5,37},{6,102},{7,39},{8,104},... | collective-permute-start | bytes 3145736 | tf_op jit(solution)/shard_map/ppermute | solution.py:273
  67.0 1.4 %collective-permute-start.14 = (bf16[2,1024,128]{2,1,0:T(8,128)(2,1)S(1)}, bf16[2,1024,128]{2,1,0:T(8,128)(2,1)S(1)}, u32[]{:S(2)}, u32[]{:S(2)}) collective-permute-start(bf16[2,1024,128]{2,1,0:T(8,128)(2,1)S(1)} %collective-permute-done.10.refs_9_.refs_11_), channel_id=1, source_target_pairs={{0,8},{1,25},{2,10},{3,27},{4,12},{5,29},{6,14},{7,31},{8,0},{9,17... | collective-permute-start | bytes 1572872 | tf_op jit(solution)/shard_map/ppermute | solution.py:273
  69.2 6.9 %product.3.refs_19_ = f32[4,16,128,128]{3,2,1,0:T(8,128)S(1)} custom-call(s32[5]{0:T(128)S(1)} %stack.23.place_ref, bf16[256,1024]{1,0:T(8,128)(2,1)} %get-tuple-element.17.refs_0_, bf16[256,1024]{1,0:T(8,128)(2,1)} %collective-permute-done.refs_1_, bf16[256,1024]{1,0:T(8,128)(2,1)S(1)} %collective-permute-done.1.refs_2_, ...), custom_call_target="tpu_custom_call" | custom-call | flops 8000000000 | bytes 1048576 | tf_op jit(solution)/shard_map/product/pallas_call | solution.py:246
  76.5 5.3 %collective-permute-done.14.refs_15_ = bf16[2,1024,128]{2,1,0:T(8,128)(2,1)S(1)} collective-permute-done((bf16[2,1024,128]{2,1,0:T(8,128)(2,1)S(1)}, bf16[2,1024,128]{2,1,0:T(8,128)(2,1)S(1)}, u32[]{:S(2)}, u32[]{:S(2)}) %collective-permute-start.14) | collective-permute-done | bytes 524320 | tf_op jit(solution)/shard_map/ppermute | solution.py:273
  81.9 1.2 %collective-permute-done.13.refs_14_ = bf16[2,1024,128]{2,1,0:T(8,128)(2,1)S(1)} collective-permute-done((bf16[2,1024,128]{2,1,0:T(8,128)(2,1)S(1)}, bf16[2,1024,128]{2,1,0:T(8,128)(2,1)S(1)}, u32[]{:S(2)}, u32[]{:S(2)}) %collective-permute-start.13) | collective-permute-done | bytes 524320 | tf_op jit(solution)/shard_map/ppermute | solution.py:273
  83.2 1.5 %collective-permute-start.15 = (bf16[4,1024,128]{2,1,0:T(8,128)(2,1)S(1)}, bf16[4,1024,128]{2,1,0:T(8,128)(2,1)S(1)}, u32[]{:S(2)}, u32[]{:S(2)}) collective-permute-start(bf16[4,1024,128]{2,1,0:T(8,128)(2,1)S(1)} %pad_maximum_fusion), channel_id=1, source_target_pairs={{0,96},{1,33},{2,98},{3,35},{4,100},{5,37},{6,102},{7,39},{8,104},... | collective-permute-start | bytes 3145736 | tf_op jit(solution)/shard_map/ppermute | solution.py:273
  84.8 1.8 %collective-permute-start.16 = (bf16[4,1024,128]{2,1,0:T(8,128)(2,1)S(1)}, bf16[4,1024,128]{2,1,0:T(8,128)(2,1)S(1)}, u32[]{:S(2)}, u32[]{:S(2)}) collective-permute-start(bf16[4,1024,128]{2,1,0:T(8,128)(2,1)S(1)} %pad_maximum_fusion.1), channel_id=1, source_target_pairs={{0,24},{1,9},{2,26},{3,11},{4,28},{5,13},{6,30},{7,15},{8,16},{9,1... | collective-permute-start | bytes 3145736 | tf_op jit(solution)/shard_map/ppermute | solution.py:273
  86.8 14.9 %product.4.refs_11_ = f32[4,16,128,128]{3,2,1,0:T(8,128)S(1)} custom-call(s32[5]{0:T(128)S(1)} %stack.23.place_ref, bf16[256,1024]{1,0:T(8,128)(2,1)} %get-tuple-element.17.refs_0_, bf16[256,1024]{1,0:T(8,128)(2,1)} %collective-permute-done.refs_1_, bf16[256,1024]{1,0:T(8,128)(2,1)S(1)} %collective-permute-done.1.refs_2_, ...), custom_call_target="tpu_custom_call" | custom-call | flops 8000000000 | bytes 1048576 | tf_op jit(solution)/shard_map/product/pallas_call | solution.py:246
  101.8 11.4 %product.5 = bf16[64,128,128]{2,1,0:T(8,128)(2,1)} custom-call(s32[5]{0:T(128)S(1)} %stack.23.place_ref, bf16[256,1024]{1,0:T(8,128)(2,1)} %get-tuple-element.17.refs_0_, bf16[256,1024]{1,0:T(8,128)(2,1)} %collective-permute-done.refs_1_, bf16[256,1024]{1,0:T(8,128)(2,1)S(1)} %collective-permute-done.1.refs_2_, ...), custom_call_target="tpu_custom_call" | custom-call | flops 80000000 | bytes 1048576 | tf_op jit(solution)/shard_map/product/pallas_call | solution.py:246
  (56 shorter events, 7.0 us)
Async XLA Ops:
  0.0 18.9 %copy-start.6 = (bf16[1024,128]{1,0:T(8,128)(2,1)S(1)}, bf16[1024,128]{1,0:T(8,128)(2,1)}, u32[]{:S(2)}) copy-start(bf16[1024,128]{1,0:T(8,128)(2,1)} %param.19) | copy-start | bytes 786436
  0.0 19.1 %copy-start.7 = (s32[32,2]{0,1:T(2,128)S(1)}, s32[32,2]{0,1:T(2,128)}, u32[]{:S(2)}) copy-start(s32[32,2]{0,1:T(2,128)} %constant.61.clone) | copy-start | bytes 772
  0.0 19.1 %copy-start.8 = (s32[32,2]{0,1:T(2,128)S(1)}, s32[32,2]{0,1:T(2,128)}, u32[]{:S(2)}) copy-start(s32[32,2]{0,1:T(2,128)} %constant.60.clone) | copy-start | bytes 772
  7.7 30.4 %all-to-all-start = ((bf16[128,8,512]{2,1,0:T(8,128)(2,1)}), bf16[128,8,512]{2,1,0:T(8,128)(2,1)S(1)}, u32[]{:S(2)}, u32[]{:S(2)}) async-start(bf16[128,8,512]{2,1,0:T(8,128)(2,1)} %bitcast.23), calls=%async_computation | async-start | bytes 2097152 | tf_op jit(solution)/shard_map/all_to_all | solution.py:319
  39.3 6.5 %collective-permute-start.8 = (bf16[1,1024,128]{2,1,0:T(8,128)(2,1)S(1)}, bf16[1,1024,128]{2,1,0:T(8,128)(2,1)S(1)}, u32[]{:S(2)}, u32[]{:S(2)}) collective-permute-start(bf16[1,1024,128]{2,1,0:T(8,128)(2,1)S(1)} %get-tuple-element.27), channel_id=1, source_target_pairs={{0,32},{1,97},{2,34},{3,99},{4,36},{5,101},{6,38},{7,103},{8,40},{... | collective-permute-start | bytes 786440 | tf_op jit(solution)/shard_map/ppermute | solution.py:273
  40.0 7.7 %collective-permute-start.7 = (bf16[1,1024,128]{2,1,0:T(8,128)(2,1)S(1)}, bf16[1,1024,128]{2,1,0:T(8,128)(2,1)S(1)}, u32[]{:S(2)}, u32[]{:S(2)}) collective-permute-start(bf16[1,1024,128]{2,1,0:T(8,128)(2,1)S(1)} %get-tuple-element.28), channel_id=1, source_target_pairs={{0,8},{1,25},{2,10},{3,27},{4,12},{5,29},{6,14},{7,31},{8,0},{9,17... | collective-permute-start | bytes 786440 | tf_op jit(solution)/shard_map/ppermute | solution.py:273
  40.7 14.7 %collective-permute-start.3 = (bf16[256,1024]{1,0:T(8,128)(2,1)}, bf16[256,1024]{1,0:T(8,128)(2,1)S(1)}, u32[]{:S(2)}, u32[]{:S(2)}) collective-permute-start(bf16[256,1024]{1,0:T(8,128)(2,1)} %get-tuple-element.17.refs_0_), channel_id=1, source_target_pairs={{0,6},{1,7},{2,4},{3,5},{4,2},{5,3},{6,0},{7,1},{8,14},{9,15},{10,... | collective-permute-start | bytes 1572872 | tf_op jit(solution)/shard_map/ppermute | solution.py:273
  40.7 14.9 %collective-permute-start.1 = (bf16[256,1024]{1,0:T(8,128)(2,1)}, bf16[256,1024]{1,0:T(8,128)(2,1)S(1)}, u32[]{:S(2)}, u32[]{:S(2)}) collective-permute-start(bf16[256,1024]{1,0:T(8,128)(2,1)} %get-tuple-element.17.refs_0_), channel_id=1, source_target_pairs={{0,2},{1,3},{2,0},{3,1},{4,6},{5,7},{6,4},{7,5},{8,10},{9,11},{10,... | collective-permute-start | bytes 1572872 | tf_op jit(solution)/shard_map/ppermute | solution.py:273
  46.5 10.5 %collective-permute-start.10 = (bf16[2,1024,128]{2,1,0:T(8,128)(2,1)S(1)}, bf16[2,1024,128]{2,1,0:T(8,128)(2,1)S(1)}, u32[]{:S(2)}, u32[]{:S(2)}) collective-permute-start(bf16[2,1024,128]{2,1,0:T(8,128)(2,1)S(1)} %pad_maximum_fusion.5.refs_7_.refs_9_), channel_id=1, source_target_pairs={{0,96},{1,33},{2,98},{3,35},{4,100},{5,37},{6,102},{7,39},{8,104},... | collective-permute-start | bytes 1572872 | tf_op jit(solution)/shard_map/ppermute | solution.py:273
  47.8 10.9 %collective-permute-start.9 = (bf16[2,1024,128]{2,1,0:T(8,128)(2,1)S(1)}, bf16[2,1024,128]{2,1,0:T(8,128)(2,1)S(1)}, u32[]{:S(2)}, u32[]{:S(2)}) collective-permute-start(bf16[2,1024,128]{2,1,0:T(8,128)(2,1)S(1)} %pad_maximum_fusion.4.refs_6_.refs_8_), channel_id=1, source_target_pairs={{0,24},{1,9},{2,26},{3,11},{4,28},{5,13},{6,30},{7,15},{8,16},{9,1... | collective-permute-start | bytes 1572872 | tf_op jit(solution)/shard_map/ppermute | solution.py:273
  48.5 12.4 %collective-permute-start = (bf16[256,1024]{1,0:T(8,128)(2,1)}, bf16[256,1024]{1,0:T(8,128)(2,1)}, u32[]{:S(2)}, u32[]{:S(2)}) collective-permute-start(bf16[256,1024]{1,0:T(8,128)(2,1)} %get-tuple-element.17.refs_0_), channel_id=1, source_target_pairs={{0,1},{1,0},{2,3},{3,2},{4,5},{5,4},{6,7},{7,6},{8,9},{9,8},{10,11... | collective-permute-start | bytes 1572872 | tf_op jit(solution)/shard_map/ppermute | solution.py:273
  55.4 9.2 %collective-permute-start.12 = (bf16[2,1024,128]{2,1,0:T(8,128)(2,1)S(1)}, bf16[2,1024,128]{2,1,0:T(8,128)(2,1)S(1)}, u32[]{:S(2)}, u32[]{:S(2)}) collective-permute-start(bf16[2,1024,128]{2,1,0:T(8,128)(2,1)S(1)} %pad_maximum_fusion.5.refs_7_.refs_9_), channel_id=1, source_target_pairs={{0,8},{1,25},{2,10},{3,27},{4,12},{5,29},{6,14},{7,31},{8,0},{9,17... | collective-permute-start | bytes 1572872 | tf_op jit(solution)/shard_map/ppermute | solution.py:273
  55.5 10.9 %collective-permute-start.11 = (bf16[2,1024,128]{2,1,0:T(8,128)(2,1)S(1)}, bf16[2,1024,128]{2,1,0:T(8,128)(2,1)S(1)}, u32[]{:S(2)}, u32[]{:S(2)}) collective-permute-start(bf16[2,1024,128]{2,1,0:T(8,128)(2,1)S(1)} %pad_maximum_fusion.4.refs_6_.refs_8_), channel_id=1, source_target_pairs={{0,32},{1,97},{2,34},{3,99},{4,36},{5,101},{6,38},{7,103},{8,40},{... | collective-permute-start | bytes 1572872 | tf_op jit(solution)/shard_map/ppermute | solution.py:273
  57.0 10.0 %collective-permute-start.4 = (bf16[256,1024]{1,0:T(8,128)(2,1)S(1)}, bf16[256,1024]{1,0:T(8,128)(2,1)S(1)}, u32[]{:S(2)}, u32[]{:S(2)}) collective-permute-start(bf16[256,1024]{1,0:T(8,128)(2,1)S(1)} %collective-permute-done.3.refs_4_), channel_id=1, source_target_pairs={{0,1},{1,0},{2,3},{3,2},{4,5},{5,4},{6,7},{7,6},{8,9},{9,8},{10,11... | collective-permute-start | bytes 1572872 | tf_op jit(solution)/shard_map/ppermute | solution.py:273
  58.6 9.8 %collective-permute-start.2 = (bf16[256,1024]{1,0:T(8,128)(2,1)S(1)}, bf16[256,1024]{1,0:T(8,128)(2,1)S(1)}, u32[]{:S(2)}, u32[]{:S(2)}) collective-permute-start(bf16[256,1024]{1,0:T(8,128)(2,1)S(1)} %collective-permute-done.1.refs_2_), channel_id=1, source_target_pairs={{0,1},{1,0},{2,3},{3,2},{4,5},{5,4},{6,7},{7,6},{8,9},{9,8},{10,11... | collective-permute-start | bytes 1572872 | tf_op jit(solution)/shard_map/ppermute | solution.py:273
  61.0 15.1 %collective-permute-start.5 = (bf16[256,1024]{1,0:T(8,128)(2,1)S(1)}, bf16[256,1024]{1,0:T(8,128)(2,1)S(1)}, u32[]{:S(2)}, u32[]{:S(2)}) collective-permute-start(bf16[256,1024]{1,0:T(8,128)(2,1)S(1)} %broadcast_select_fusion), channel_id=1, source_target_pairs={{0,6},{1,3},{2,4},{3,1},{4,2},{5,7},{6,0},{7,5},{8,14},{9,11},{10,... | collective-permute-start | bytes 1572872 | tf_op jit(solution)/shard_map/ppermute | solution.py:273
  64.6 22.0 %collective-permute-start.17 = (bf16[4,1024,128]{2,1,0:T(8,128)(2,1)S(1)}, bf16[4,1024,128]{2,1,0:T(8,128)(2,1)S(1)}, u32[]{:S(2)}, u32[]{:S(2)}) collective-permute-start(bf16[4,1024,128]{2,1,0:T(8,128)(2,1)S(1)} %pad_maximum_fusion.2), channel_id=1, source_target_pairs={{0,96},{1,33},{2,98},{3,35},{4,100},{5,37},{6,102},{7,39},{8,104},... | collective-permute-start | bytes 3145736 | tf_op jit(solution)/shard_map/ppermute | solution.py:273
  66.4 20.4 %collective-permute-start.18 = (bf16[4,1024,128]{2,1,0:T(8,128)(2,1)S(1)}, bf16[4,1024,128]{2,1,0:T(8,128)(2,1)S(1)}, u32[]{:S(2)}, u32[]{:S(2)}) collective-permute-start(bf16[4,1024,128]{2,1,0:T(8,128)(2,1)S(1)} %pad_maximum_fusion.3), channel_id=1, source_target_pairs={{0,24},{1,9},{2,26},{3,11},{4,28},{5,13},{6,30},{7,15},{8,16},{9,1... | collective-permute-start | bytes 3145736 | tf_op jit(solution)/shard_map/ppermute | solution.py:273
  67.0 14.9 %collective-permute-start.14 = (bf16[2,1024,128]{2,1,0:T(8,128)(2,1)S(1)}, bf16[2,1024,128]{2,1,0:T(8,128)(2,1)S(1)}, u32[]{:S(2)}, u32[]{:S(2)}) collective-permute-start(bf16[2,1024,128]{2,1,0:T(8,128)(2,1)S(1)} %collective-permute-done.10.refs_9_.refs_11_), channel_id=1, source_target_pairs={{0,8},{1,25},{2,10},{3,27},{4,12},{5,29},{6,14},{7,31},{8,0},{9,17... | collective-permute-start | bytes 1572872 | tf_op jit(solution)/shard_map/ppermute | solution.py:273
  68.4 14.7 %collective-permute-start.13 = (bf16[2,1024,128]{2,1,0:T(8,128)(2,1)S(1)}, bf16[2,1024,128]{2,1,0:T(8,128)(2,1)S(1)}, u32[]{:S(2)}, u32[]{:S(2)}) collective-permute-start(bf16[2,1024,128]{2,1,0:T(8,128)(2,1)S(1)} %collective-permute-done.9.refs_8_.refs_10_), channel_id=1, source_target_pairs={{0,32},{1,97},{2,34},{3,99},{4,36},{5,101},{6,38},{7,103},{8,40},{... | collective-permute-start | bytes 1572872 | tf_op jit(solution)/shard_map/ppermute | solution.py:273
  76.1 10.5 %collective-permute-start.6 = (bf16[256,1024]{1,0:T(8,128)(2,1)S(1)}, bf16[256,1024]{1,0:T(8,128)(2,1)S(1)}, u32[]{:S(2)}, u32[]{:S(2)}) collective-permute-start(bf16[256,1024]{1,0:T(8,128)(2,1)S(1)} %collective-permute-done.5.refs_6_), channel_id=1, source_target_pairs={{0,1},{1,0},{2,3},{3,2},{4,5},{5,4},{6,7},{7,6},{8,9},{9,8},{10,11... | collective-permute-start | bytes 1572872 | tf_op jit(solution)/shard_map/ppermute | solution.py:273
  83.2 18.6 %collective-permute-start.15 = (bf16[4,1024,128]{2,1,0:T(8,128)(2,1)S(1)}, bf16[4,1024,128]{2,1,0:T(8,128)(2,1)S(1)}, u32[]{:S(2)}, u32[]{:S(2)}) collective-permute-start(bf16[4,1024,128]{2,1,0:T(8,128)(2,1)S(1)} %pad_maximum_fusion), channel_id=1, source_target_pairs={{0,96},{1,33},{2,98},{3,35},{4,100},{5,37},{6,102},{7,39},{8,104},... | collective-permute-start | bytes 3145736 | tf_op jit(solution)/shard_map/ppermute | solution.py:273
  84.8 17.0 %copy-start = (bf16[64,128,128]{2,1,0:T(8,128)(2,1)S(1)}, bf16[64,128,128]{2,1,0:T(8,128)(2,1)}, u32[]{:S(2)}) copy-start(bf16[64,128,128]{2,1,0:T(8,128)(2,1)} %refs_12_.1) | copy-start | bytes 6291460
  84.8 17.0 %collective-permute-start.16 = (bf16[4,1024,128]{2,1,0:T(8,128)(2,1)S(1)}, bf16[4,1024,128]{2,1,0:T(8,128)(2,1)S(1)}, u32[]{:S(2)}, u32[]{:S(2)}) collective-permute-start(bf16[4,1024,128]{2,1,0:T(8,128)(2,1)S(1)} %pad_maximum_fusion.1), channel_id=1, source_target_pairs={{0,24},{1,9},{2,26},{3,11},{4,28},{5,13},{6,30},{7,15},{8,16},{9,1... | collective-permute-start | bytes 3145736 | tf_op jit(solution)/shard_map/ppermute | solution.py:273
  (5 other events, 34.3 us)

commit v4 on v3

--- a/solution.py
+++ b/solution.py
@@ -56,7 +56,10 @@
     for c in range(8):
         rows = right[c].astype(jnp.bfloat16).reshape(16, 2, 8, 128)
         for d in range(2):
-            out_ref[:, c, :, 256 + d * 128 : 256 + (d + 1) * 128] = rows[:, d]
+            at = 256 + d * 256
+            partner = mask_of(0, c % 2) * (4 if d else 1)
+            out_ref[:, c, :, at : at + 128] = rows[:, d]
+            out_ref[:, c, :, at + 128 : at + 256] = jnp.stack([rows[r ^ partner, d] for r in range(16)])
 
 
 def project(x, gain, offset, first, first_offset, second, second_offset):
@@ -65,7 +68,7 @@
         project_kernel,
         in_specs=[pl.BlockSpec(memory_space=pl.ANY)] + [whole] * 6,
         out_specs=whole,
-        out_shape=jax.ShapeDtypeStruct((16, 8, 8, 512), jnp.bfloat16),
+        out_shape=jax.ShapeDtypeStruct((16, 8, 8, 768), jnp.bfloat16),
         scratch_shapes=[
             pltpu.VMEM((8, 1024, 256), jnp.bfloat16),
             pltpu.VMEM((2048, 128), jnp.float32),
@@ -85,12 +88,12 @@
     )
 
 
-def split_kernel(x_ref, left_ref, right_ref):
+def split_kernel(x_ref, left_ref, *right_refs):
     for n in range(8):
         at = n * 128
         left_ref[:, at : at + 128] = jnp.transpose(x_ref[at : at + 128, :256])
-    for d in range(2):
-        right_ref[d] = x_ref[:, 256 + d * 128 : 256 + (d + 1) * 128]
+    for n in range(4):
+        right_refs[n // 2][n % 2] = x_ref[:, 256 + n * 128 : 256 + (n + 1) * 128]
 
 
 def split(received):
@@ -98,6 +101,7 @@
         split_kernel,
         out_shape=(
             jax.ShapeDtypeStruct((256, 1024), jnp.bfloat16),
+            jax.ShapeDtypeStruct((2, 1024, 128), jnp.bfloat16),
             jax.ShapeDtypeStruct((2, 1024, 128), jnp.bfloat16),
         ),
         compiler_params=pltpu.CompilerParams(vmem_limit_bytes=16 * MIB),
@@ -315,7 +319,7 @@
         first_factor_offset,
         second_factor_matrix,
         second_factor_offset,
-    ).reshape(128, 8, 512)
+    ).reshape(128, 8, 768)
     received = lax.all_to_all(projected, ("row", "col"), split_axis=0, concat_axis=0, tiled=True)
 
     order = np.array(
@@ -336,7 +340,7 @@
 
     place = jnp.stack([z, z ^ 1, z ^ 3, z ^ 2, core]).astype(jnp.int32)
     received, weights, place = lax.optimization_barrier((received, weights, place))
-    own, right = split(received.reshape(1024, 512))
+    own, *two = split(received.reshape(1024, 768))
 
     def send(blocks, step):
         return [permute(blocks[part], functools.partial(hop, part, step)) for part in range(2)]
@@ -344,8 +348,6 @@
     def join(first, second):
         return [jnp.concatenate(both, axis=0) for both in zip(first, second)]
 
-    block = [right[part : part + 1] for part in range(2)]
-    two = join(block, send(block, 0))
     two_more = send(two, 1)
     third = [send(two, 2), send(two_more, 2)]
     fourth = send(join(two, two_more), 3)

time: 114 us -> 115 us (level)
  waiting for transfers between devices: 39.9 us -> 44.4 us
  local copies, waits for them, and re-layouts: 2.67 us -> 0.97 us
    all_to_all x1, waiting for transfers between devices: 17.5 us -> 23.8 us  [per_device(): lax.all_to_all(projected, ('row', 'col'), split_axis=0, concat_axis=0, ti...]
    ppermute x19 -> x17, waiting for transfers between devices: 22.4 us -> 20.6 us  [permute(): return lax.ppermute(value, ('row', 'col'), pairs)]
    ppermute x19 -> x17, starting transfers between devices: 13.7 us -> 12.7 us  [permute(): return lax.ppermute(value, ('row', 'col'), pairs)]
    concatenate x6 -> x4, other arithmetic: 2.55 us -> 2.45 us  [join(): return [jnp.concatenate(both, axis=0) for both in zip(first, second)]]
  transfers between devices with their start and end apart: 20 -> 18, of which waited for: 9 -> 6; matrix products, arithmetic and copies ran while one was open for 5% -> 3% of each run, Pallas kernels for 19% -> 19%
where the time goes in v4:
time: 115 us
  waiting for transfers between devices  44.4 us (39%)
  Pallas kernels  42.4 us (37%)
  starting transfers between devices  23.9 us (21%)
  other arithmetic  2.66 us (2%)
    pallas_call x3, Pallas kernels, product(): pl.pallas_call(functools.partial(product_kernel, low, high, right_at, sta...  33.3 us
    all_to_all x1, waiting for transfers between devices, per_device(): lax.all_to_all(projected, ('row', 'col'), split_axis=0, concat_axis=0, ti...  23.8 us
    ppermute x17, waiting for transfers between devices, permute(): return lax.ppermute(value, ('row', 'col'), pairs)  20.6 us
    ppermute x17, starting transfers between devices, permute(): return lax.ppermute(value, ('row', 'col'), pairs)  12.7 us
    all_to_all x1, starting transfers between devices, per_device(): lax.all_to_all(projected, ('row', 'col'), split_axis=0, concat_axis=0, ti...  11.1 us
    pallas_call x1, Pallas kernels, project(): pl.pallas_call(project_kernel, in_specs=[pl.BlockSpec(memory_space=pl.ANY...  7.89 us
    concatenate x4, other arithmetic, join(): return [jnp.concatenate(both, axis=0) for both in zip(first, second)]  2.45 us
  transfers between devices with their start and end apart: 18, of which 6 were waited for; matrix products, arithmetic and copies ran while one was open for 3% of the time, Pallas kernels for 19%

profile of v4, /device:TPU:0, one launch (start us, length us, event | category | flops | bytes accessed | tf_op | source)
XLA Modules:
  0.0 114.7 jit_solution(6609948532454057151)
XLA Ops:
  0.0 7.9 %project.1 = bf16[16,8,8,768]{3,2,1,0:T(8,128)(2,1)} custom-call(bf16[8,1024,256]{2,1,0:T(8,128)(2,1)} %x_ref.1, f32[1,256]{1,0:T(1,128)} %bitcast.29, f32[1,256]{1,0:T(1,128)} %bitcast.30, bf16[32,256]{1,0:T(8,128)(2,1)} %bitcast.26, f32[1,32]{1,0:T(1,128)} %bitcast.31, bf16[32,256]{1,0:T(8,128)(2,1)} %bitcast.27, f32[1,32]{1,0:T(1,128)} %bitcast.32), custom_call_target="tpu_custom_call" | custom-call | tf_op jit(solution)/shard_map/project/pallas_call | solution.py:67
  7.9 11.1 %all-to-all-start = ((bf16[128,8,768]{2,1,0:T(8,128)(2,1)}), bf16[128,8,768]{2,1,0:T(8,128)(2,1)S(1)}, u32[]{:S(2)}, u32[]{:S(2)}) async-start(bf16[128,8,768]{2,1,0:T(8,128)(2,1)} %bitcast.23), calls=%async_computation | async-start | bytes 3145728 | tf_op jit(solution)/shard_map/all_to_all | solution.py:323
  19.3 0.6 gather_fusion
  20.1 23.8 %all-to-all-done = bf16[128,8,768]{2,1,0:T(8,128)(2,1)S(1)} async-done(((bf16[128,8,768]{2,1,0:T(8,128)(2,1)}), bf16[128,8,768]{2,1,0:T(8,128)(2,1)S(1)}, u32[]{:S(2)}, u32[]{:S(2)}) %all-to-all-start) | async-done | bytes 1572896 | tf_op jit(solution)/shard_map/all_to_all | solution.py:323
  44.0 1.1 split.1
  45.1 1.1 collective-permute-start.7
  46.2 0.8 collective-permute-start.8
  46.9 1.0 collective-permute-start.3
  48.2 7.3 %collective-permute-done.7.refs_8_.refs_10_ = bf16[2,1024,128]{2,1,0:T(8,128)(2,1)S(1)} collective-permute-done((bf16[2,1024,128]{2,1,0:T(8,128)(2,1)S(1)}, bf16[2,1024,128]{2,1,0:T(8,128)(2,1)S(1)}, u32[]{:S(2)}, u32[]{:S(2)}) %collective-permute-start.7) | collective-permute-done | bytes 524320 | tf_op jit(solution)/shard_map/ppermute | solution.py:277
  55.5 4.9 %collective-permute-done.8.refs_9_.refs_11_ = bf16[2,1024,128]{2,1,0:T(8,128)(2,1)} collective-permute-done((bf16[2,1024,128]{2,1,0:T(8,128)(2,1)S(1)}, bf16[2,1024,128]{2,1,0:T(8,128)(2,1)}, u32[]{:S(2)}, u32[]{:S(2)}) %collective-permute-start.8) | collective-permute-done | bytes 524320 | tf_op jit(solution)/shard_map/ppermute | solution.py:277
  60.5 0.4 collective-permute-start.4
  61.0 1.1 pad_maximum_fusion.3
  62.3 2.4 %collective-permute-start.5 = (bf16[256,1024]{1,0:T(8,128)(2,1)S(1)}, bf16[256,1024]{1,0:T(8,128)(2,1)S(1)}, u32[]{:S(2)}, u32[]{:S(2)}) collective-permute-start(bf16[256,1024]{1,0:T(8,128)(2,1)S(1)} %broadcast_select_fusion), channel_id=1, source_target_pairs={{0,6},{1,3},{2,4},{3,1},{4,2},{5,7},{6,0},{7,5},{8,14},{9,11},{10,... | collective-permute-start | bytes 1572872 | tf_op jit(solution)/shard_map/ppermute | solution.py:277
  64.7 1.3 %collective-permute-start.15 = (bf16[4,1024,128]{2,1,0:T(8,128)(2,1)S(1)}, bf16[4,1024,128]{2,1,0:T(8,128)(2,1)S(1)}, u32[]{:S(2)}, u32[]{:S(2)}) collective-permute-start(bf16[4,1024,128]{2,1,0:T(8,128)(2,1)S(1)} %pad_maximum_fusion.2), channel_id=1, source_target_pairs={{0,96},{1,33},{2,98},{3,35},{4,100},{5,37},{6,102},{7,39},{8,104},... | collective-permute-start | bytes 3145736 | tf_op jit(solution)/shard_map/ppermute | solution.py:277
  66.0 1.7 %collective-permute-start.16 = (bf16[4,1024,128]{2,1,0:T(8,128)(2,1)S(1)}, bf16[4,1024,128]{2,1,0:T(8,128)(2,1)S(1)}, u32[]{:S(2)}, u32[]{:S(2)}) collective-permute-start(bf16[4,1024,128]{2,1,0:T(8,128)(2,1)S(1)} %pad_maximum_fusion.3), channel_id=1, source_target_pairs={{0,24},{1,9},{2,26},{3,11},{4,28},{5,13},{6,30},{7,15},{8,16},{9,1... | collective-permute-start | bytes 3145736 | tf_op jit(solution)/shard_map/ppermute | solution.py:277
  67.7 0.3 collective-permute-start.12
  67.9 6.8 %product.3.refs_19_ = f32[4,16,128,128]{3,2,1,0:T(8,128)S(1)} custom-call(s32[5]{0:T(128)S(1)} %stack.23.place_ref, bf16[256,1024]{1,0:T(8,128)(2,1)} %get-tuple-element.18.refs_0_, bf16[256,1024]{1,0:T(8,128)(2,1)S(1)} %collective-permute-done.refs_1_, bf16[256,1024]{1,0:T(8,128)(2,1)S(1)} %collective-permute-done.1.refs_2_, ...), custom_call_target="tpu_custom_call" | custom-call | flops 8000000000 | bytes 1048576 | tf_op jit(solution)/shard_map/product/pallas_call | solution.py:250
  74.7 7.8 %collective-permute-done.11.refs_14_ = bf16[2,1024,128]{2,1,0:T(8,128)(2,1)S(1)} collective-permute-done((bf16[2,1024,128]{2,1,0:T(8,128)(2,1)S(1)}, bf16[2,1024,128]{2,1,0:T(8,128)(2,1)S(1)}, u32[]{:S(2)}, u32[]{:S(2)}) %collective-permute-start.11) | collective-permute-done | bytes 524320 | tf_op jit(solution)/shard_map/ppermute | solution.py:277
  82.5 0.5 collective-permute-done.12.refs_15_
  83.0 1.1 pad_maximum_fusion
  84.1 1.6 %collective-permute-start.13 = (bf16[4,1024,128]{2,1,0:T(8,128)(2,1)S(1)}, bf16[4,1024,128]{2,1,0:T(8,128)(2,1)S(1)}, u32[]{:S(2)}, u32[]{:S(2)}) collective-permute-start(bf16[4,1024,128]{2,1,0:T(8,128)(2,1)S(1)} %pad_maximum_fusion), channel_id=1, source_target_pairs={{0,96},{1,33},{2,98},{3,35},{4,100},{5,37},{6,102},{7,39},{8,104},... | collective-permute-start | bytes 3145736 | tf_op jit(solution)/shard_map/ppermute | solution.py:277
  85.8 2.1 %collective-permute-start.14 = (bf16[4,1024,128]{2,1,0:T(8,128)(2,1)S(1)}, bf16[4,1024,128]{2,1,0:T(8,128)(2,1)S(1)}, u32[]{:S(2)}, u32[]{:S(2)}) collective-permute-start(bf16[4,1024,128]{2,1,0:T(8,128)(2,1)S(1)} %pad_maximum_fusion.1), channel_id=1, source_target_pairs={{0,24},{1,9},{2,26},{3,11},{4,28},{5,13},{6,30},{7,15},{8,16},{9,1... | collective-permute-start | bytes 3145736 | tf_op jit(solution)/shard_map/ppermute | solution.py:277
  87.9 15.1 %product.4.refs_11_ = f32[4,16,128,128]{3,2,1,0:T(8,128)S(1)} custom-call(s32[5]{0:T(128)S(1)} %stack.23.place_ref, bf16[256,1024]{1,0:T(8,128)(2,1)} %get-tuple-element.18.refs_0_, bf16[256,1024]{1,0:T(8,128)(2,1)S(1)} %collective-permute-done.refs_1_, bf16[256,1024]{1,0:T(8,128)(2,1)S(1)} %collective-permute-done.1.refs_2_, ...), custom_call_target="tpu_custom_call" | custom-call | flops 8000000000 | bytes 1048576 | tf_op jit(solution)/shard_map/product/pallas_call | solution.py:250
  103.1 11.5 %product.5 = bf16[64,128,128]{2,1,0:T(8,128)(2,1)} custom-call(s32[5]{0:T(128)S(1)} %stack.23.place_ref, bf16[256,1024]{1,0:T(8,128)(2,1)} %get-tuple-element.18.refs_0_, bf16[256,1024]{1,0:T(8,128)(2,1)S(1)} %collective-permute-done.refs_1_, bf16[256,1024]{1,0:T(8,128)(2,1)S(1)} %collective-permute-done.1.refs_2_, ...), custom_call_target="tpu_custom_call" | custom-call | flops 80000000 | bytes 1048576 | tf_op jit(solution)/shard_map/product/pallas_call | solution.py:250
  (41 shorter events, 1.1 us)
Async XLA Ops:
  7.9 11.2 %copy-start.2 = (bf16[1024,128]{1,0:T(8,128)(2,1)S(1)}, bf16[1024,128]{1,0:T(8,128)(2,1)}, u32[]{:S(2)}) copy-start(bf16[1024,128]{1,0:T(8,128)(2,1)} %param.19) | copy-start | bytes 786436
  7.9 11.4 %copy-start.3 = (s32[32,2]{0,1:T(2,128)S(1)}, s32[32,2]{0,1:T(2,128)}, u32[]{:S(2)}) copy-start(s32[32,2]{0,1:T(2,128)} %constant.61.clone) | copy-start | bytes 772
  7.9 11.4 %copy-start.4 = (s32[32,2]{0,1:T(2,128)S(1)}, s32[32,2]{0,1:T(2,128)}, u32[]{:S(2)}) copy-start(s32[32,2]{0,1:T(2,128)} %constant.60.clone) | copy-start | bytes 772
  7.9 36.0 %all-to-all-start = ((bf16[128,8,768]{2,1,0:T(8,128)(2,1)}), bf16[128,8,768]{2,1,0:T(8,128)(2,1)S(1)}, u32[]{:S(2)}, u32[]{:S(2)}) async-start(bf16[128,8,768]{2,1,0:T(8,128)(2,1)} %bitcast.23), calls=%async_computation | async-start | bytes 3145728 | tf_op jit(solution)/shard_map/all_to_all | solution.py:323
  45.1 10.4 %collective-permute-start.7 = (bf16[2,1024,128]{2,1,0:T(8,128)(2,1)S(1)}, bf16[2,1024,128]{2,1,0:T(8,128)(2,1)S(1)}, u32[]{:S(2)}, u32[]{:S(2)}) collective-permute-start(bf16[2,1024,128]{2,1,0:T(8,128)(2,1)S(1)} %get-tuple-element.19.refs_6_.refs_8_), channel_id=1, source_target_pairs={{0,24},{1,9},{2,26},{3,11},{4,28},{5,13},{6,30},{7,15},{8,16},{9,1... | collective-permute-start | bytes 1572872 | tf_op jit(solution)/shard_map/ppermute | solution.py:277
  46.2 14.2 %collective-permute-start.8 = (bf16[2,1024,128]{2,1,0:T(8,128)(2,1)S(1)}, bf16[2,1024,128]{2,1,0:T(8,128)(2,1)}, u32[]{:S(2)}, u32[]{:S(2)}) collective-permute-start(bf16[2,1024,128]{2,1,0:T(8,128)(2,1)S(1)} %get-tuple-element.20.refs_7_.refs_9_), channel_id=1, source_target_pairs={{0,96},{1,33},{2,98},{3,35},{4,100},{5,37},{6,102},{7,39},{8,104},... | collective-permute-start | bytes 1572872 | tf_op jit(solution)/shard_map/ppermute | solution.py:277
  46.9 13.5 %collective-permute-start.3 = (bf16[256,1024]{1,0:T(8,128)(2,1)}, bf16[256,1024]{1,0:T(8,128)(2,1)S(1)}, u32[]{:S(2)}, u32[]{:S(2)}) collective-permute-start(bf16[256,1024]{1,0:T(8,128)(2,1)} %get-tuple-element.18.refs_0_), channel_id=1, source_target_pairs={{0,6},{1,7},{2,4},{3,5},{4,2},{5,3},{6,0},{7,1},{8,14},{9,15},{10,... | collective-permute-start | bytes 1572872 | tf_op jit(solution)/shard_map/ppermute | solution.py:277
  47.9 13.0 %collective-permute-start.1 = (bf16[256,1024]{1,0:T(8,128)(2,1)}, bf16[256,1024]{1,0:T(8,128)(2,1)S(1)}, u32[]{:S(2)}, u32[]{:S(2)}) collective-permute-start(bf16[256,1024]{1,0:T(8,128)(2,1)} %get-tuple-element.18.refs_0_), channel_id=1, source_target_pairs={{0,2},{1,3},{2,0},{3,1},{4,6},{5,7},{6,4},{7,5},{8,10},{9,11},{10,... | collective-permute-start | bytes 1572872 | tf_op jit(solution)/shard_map/ppermute | solution.py:277
  48.0 14.3 %collective-permute-start.9 = (bf16[2,1024,128]{2,1,0:T(8,128)(2,1)S(1)}, bf16[2,1024,128]{2,1,0:T(8,128)(2,1)}, u32[]{:S(2)}, u32[]{:S(2)}) collective-permute-start(bf16[2,1024,128]{2,1,0:T(8,128)(2,1)S(1)} %get-tuple-element.19.refs_6_.refs_8_), channel_id=1, source_target_pairs={{0,32},{1,97},{2,34},{3,99},{4,36},{5,101},{6,38},{7,103},{8,40},{... | collective-permute-start | bytes 1572872 | tf_op jit(solution)/shard_map/ppermute | solution.py:277
  55.5 9.2 %collective-permute-start.10 = (bf16[2,1024,128]{2,1,0:T(8,128)(2,1)S(1)}, bf16[2,1024,128]{2,1,0:T(8,128)(2,1)S(1)}, u32[]{:S(2)}, u32[]{:S(2)}) collective-permute-start(bf16[2,1024,128]{2,1,0:T(8,128)(2,1)S(1)} %get-tuple-element.20.refs_7_.refs_9_), channel_id=1, source_target_pairs={{0,8},{1,25},{2,10},{3,27},{4,12},{5,29},{6,14},{7,31},{8,0},{9,17... | collective-permute-start | bytes 1572872 | tf_op jit(solution)/shard_map/ppermute | solution.py:277
  60.4 5.6 %collective-permute-start = (bf16[256,1024]{1,0:T(8,128)(2,1)}, bf16[256,1024]{1,0:T(8,128)(2,1)S(1)}, u32[]{:S(2)}, u32[]{:S(2)}) collective-permute-start(bf16[256,1024]{1,0:T(8,128)(2,1)} %get-tuple-element.18.refs_0_), channel_id=1, source_target_pairs={{0,1},{1,0},{2,3},{3,2},{4,5},{5,4},{6,7},{7,6},{8,9},{9,8},{10,11... | collective-permute-start | bytes 1572872 | tf_op jit(solution)/shard_map/ppermute | solution.py:277
  60.5 7.2 %collective-permute-start.4 = (bf16[256,1024]{1,0:T(8,128)(2,1)S(1)}, bf16[256,1024]{1,0:T(8,128)(2,1)S(1)}, u32[]{:S(2)}, u32[]{:S(2)}) collective-permute-start(bf16[256,1024]{1,0:T(8,128)(2,1)S(1)} %collective-permute-done.3.refs_4_), channel_id=1, source_target_pairs={{0,1},{1,0},{2,3},{3,2},{4,5},{5,4},{6,7},{7,6},{8,9},{9,8},{10,11... | collective-permute-start | bytes 1572872 | tf_op jit(solution)/shard_map/ppermute | solution.py:277
  60.9 6.8 %collective-permute-start.2 = (bf16[256,1024]{1,0:T(8,128)(2,1)S(1)}, bf16[256,1024]{1,0:T(8,128)(2,1)S(1)}, u32[]{:S(2)}, u32[]{:S(2)}) collective-permute-start(bf16[256,1024]{1,0:T(8,128)(2,1)S(1)} %collective-permute-done.1.refs_2_), channel_id=1, source_target_pairs={{0,1},{1,0},{2,3},{3,2},{4,5},{5,4},{6,7},{7,6},{8,9},{9,8},{10,11... | collective-permute-start | bytes 1572872 | tf_op jit(solution)/shard_map/ppermute | solution.py:277
  62.3 20.7 %collective-permute-start.5 = (bf16[256,1024]{1,0:T(8,128)(2,1)S(1)}, bf16[256,1024]{1,0:T(8,128)(2,1)S(1)}, u32[]{:S(2)}, u32[]{:S(2)}) collective-permute-start(bf16[256,1024]{1,0:T(8,128)(2,1)S(1)} %broadcast_select_fusion), channel_id=1, source_target_pairs={{0,6},{1,3},{2,4},{3,1},{4,2},{5,7},{6,0},{7,5},{8,14},{9,11},{10,... | collective-permute-start | bytes 1572872 | tf_op jit(solution)/shard_map/ppermute | solution.py:277
  64.7 23.3 %collective-permute-start.15 = (bf16[4,1024,128]{2,1,0:T(8,128)(2,1)S(1)}, bf16[4,1024,128]{2,1,0:T(8,128)(2,1)S(1)}, u32[]{:S(2)}, u32[]{:S(2)}) collective-permute-start(bf16[4,1024,128]{2,1,0:T(8,128)(2,1)S(1)} %pad_maximum_fusion.2), channel_id=1, source_target_pairs={{0,96},{1,33},{2,98},{3,35},{4,100},{5,37},{6,102},{7,39},{8,104},... | collective-permute-start | bytes 3145736 | tf_op jit(solution)/shard_map/ppermute | solution.py:277
  66.0 22.0 %collective-permute-start.16 = (bf16[4,1024,128]{2,1,0:T(8,128)(2,1)S(1)}, bf16[4,1024,128]{2,1,0:T(8,128)(2,1)S(1)}, u32[]{:S(2)}, u32[]{:S(2)}) collective-permute-start(bf16[4,1024,128]{2,1,0:T(8,128)(2,1)S(1)} %pad_maximum_fusion.3), channel_id=1, source_target_pairs={{0,24},{1,9},{2,26},{3,11},{4,28},{5,13},{6,30},{7,15},{8,16},{9,1... | collective-permute-start | bytes 3145736 | tf_op jit(solution)/shard_map/ppermute | solution.py:277
  67.7 14.9 %collective-permute-start.11 = (bf16[2,1024,128]{2,1,0:T(8,128)(2,1)S(1)}, bf16[2,1024,128]{2,1,0:T(8,128)(2,1)S(1)}, u32[]{:S(2)}, u32[]{:S(2)}) collective-permute-start(bf16[2,1024,128]{2,1,0:T(8,128)(2,1)S(1)} %collective-permute-done.7.refs_8_.refs_10_), channel_id=1, source_target_pairs={{0,32},{1,97},{2,34},{3,99},{4,36},{5,101},{6,38},{7,103},{8,40},{... | collective-permute-start | bytes 1572872 | tf_op jit(solution)/shard_map/ppermute | solution.py:277
  67.7 15.3 %collective-permute-start.12 = (bf16[2,1024,128]{2,1,0:T(8,128)(2,1)}, bf16[2,1024,128]{2,1,0:T(8,128)(2,1)S(1)}, u32[]{:S(2)}, u32[]{:S(2)}) collective-permute-start(bf16[2,1024,128]{2,1,0:T(8,128)(2,1)} %collective-permute-done.8.refs_9_.refs_11_), channel_id=1, source_target_pairs={{0,8},{1,25},{2,10},{3,27},{4,12},{5,29},{6,14},{7,31},{8,0},{9,17... | collective-permute-start | bytes 1572872 | tf_op jit(solution)/shard_map/ppermute | solution.py:277
  83.0 4.9 %collective-permute-start.6 = (bf16[256,1024]{1,0:T(8,128)(2,1)S(1)}, bf16[256,1024]{1,0:T(8,128)(2,1)S(1)}, u32[]{:S(2)}, u32[]{:S(2)}) collective-permute-start(bf16[256,1024]{1,0:T(8,128)(2,1)S(1)} %collective-permute-done.5.refs_6_), channel_id=1, source_target_pairs={{0,1},{1,0},{2,3},{3,2},{4,5},{5,4},{6,7},{7,6},{8,9},{9,8},{10,11... | collective-permute-start | bytes 1572872 | tf_op jit(solution)/shard_map/ppermute | solution.py:277
  84.1 18.9 %collective-permute-start.13 = (bf16[4,1024,128]{2,1,0:T(8,128)(2,1)S(1)}, bf16[4,1024,128]{2,1,0:T(8,128)(2,1)S(1)}, u32[]{:S(2)}, u32[]{:S(2)}) collective-permute-start(bf16[4,1024,128]{2,1,0:T(8,128)(2,1)S(1)} %pad_maximum_fusion), channel_id=1, source_target_pairs={{0,96},{1,33},{2,98},{3,35},{4,100},{5,37},{6,102},{7,39},{8,104},... | collective-permute-start | bytes 3145736 | tf_op jit(solution)/shard_map/ppermute | solution.py:277
  85.8 17.3 %copy-start = (bf16[64,128,128]{2,1,0:T(8,128)(2,1)S(1)}, bf16[64,128,128]{2,1,0:T(8,128)(2,1)}, u32[]{:S(2)}) copy-start(bf16[64,128,128]{2,1,0:T(8,128)(2,1)} %refs_12_.1) | copy-start | bytes 6291460
  85.8 17.3 %copy-start.1 = (f32[128]{0:T(128)S(1)}, f32[128]{0:T(128)}, u32[]{:S(2)}) copy-start(f32[128]{0:T(128)} %param.20) | copy-start | bytes 1540
  85.8 17.2 %collective-permute-start.14 = (bf16[4,1024,128]{2,1,0:T(8,128)(2,1)S(1)}, bf16[4,1024,128]{2,1,0:T(8,128)(2,1)S(1)}, u32[]{:S(2)}, u32[]{:S(2)}) collective-permute-start(bf16[4,1024,128]{2,1,0:T(8,128)(2,1)S(1)} %pad_maximum_fusion.1), channel_id=1, source_target_pairs={{0,24},{1,9},{2,26},{3,11},{4,28},{5,13},{6,30},{7,15},{8,16},{9,1... | collective-permute-start | bytes 3145736 | tf_op jit(solution)/shard_map/ppermute | solution.py:277
